TPU v7x, 512 devices: a whole 4x8x8 slice. The times are simulated.
512 devices in a mesh: depth: 8 (over z), tx: 8 (over y_hi, core), ty: 8 (over x, y_lo).
Axes of the slice: x: 4, y: 8 (y_hi: 4, y_lo: 2; y = y_hi * 2 + y_lo), z: 8, core: 2. Of those that a mesh axis runs over, the one named last changes fastest.
Arguments:
- mask: int32 [8, 512, 4096], P('tx', 'depth', 'ty'), may hold values from 0 to 1, as said below
- kernels: bfloat16 [8, 12, 64, 128], P('depth'), may hold values from -6 to 6
- weights: float32 [12], replicated, may hold values from 0.02 to 0.2
- band_rows: int32 [64], replicated, may hold values from 0 to 127, as said below
- band_cols: int32 [64], replicated, may hold values from 0 to 127, as said below
- quencher: float32 [8, 8, 512, 4096], P(None, 'tx', 'depth', 'ty'), may hold values from 0.1 to 0.6
Outputs:
- acid: float32 [8, 8, 512, 4096], P(None, 'tx', 'depth', 'ty')
- quencher_left: float32 [8, 8, 512, 4096], P(None, 'tx', 'depth', 'ty')
Inputs may be any that keep to these rules, and one draw needn't show every extreme that they name: `mask`: 0 or 1, equal on each aligned block of 2 x 2 pixels. `band_rows`: 64 distinct band indices. `band_cols`: 64 distinct band indices.
All inputs are finite; a program needn't handle non-finite values.
Results may differ from a plain program's by a relative error of at most 0.0016.
Values may be sent and summed in bfloat16 or wider, within the bound.
No kernel may reach another device: no remote copies, remote signals or barrier semaphores. Data moves between devices by JAX's collectives and lax.ppermute only.
A program may use at most 64 MiB of HBM per device.

v0:
```python
import math

import jax
import jax.numpy as jnp
from jax import lax
from jax.sharding import PartitionSpec as P

STEPS = 2


DILL_RATE = 1.0
REACT_RATE = 0.4


def padded(cells, sides, width):
    for axis, dim in sides:
        count = lax.axis_size(axis)
        head = lax.slice_in_dim(cells, 0, width, axis=dim)
        tail = lax.slice_in_dim(cells, cells.shape[dim] - width, cells.shape[dim], axis=dim)
        cells = jnp.concatenate(
            [
                lax.ppermute(tail, axis, [(i, (i + 1) % count) for i in range(count)]),
                cells,
                lax.ppermute(head, axis, [((i + 1) % count, i) for i in range(count)]),
            ],
            axis=dim,
        )
    return cells


def shortened(array):
    return jax.tree.map(lambda a: a.astype(jnp.bfloat16) if a.dtype == jnp.float32 else a, array)


def phase_table(freqs, length, offset, count):
    coords = offset + jnp.arange(count, dtype=jnp.int32)
    index = jnp.mod(coords[:, None] * freqs[None, :], length)
    angle = index.astype(jnp.float32) * (2.0 * math.pi / length)
    return (jnp.cos(angle), jnp.sin(angle))


def mask_spectrum(rows, cos_x, sin_x, cos_y, sin_y):
    band = cos_y.shape[1]
    highest = lax.Precision.HIGHEST
    summed = jnp.dot(rows, jnp.concatenate([cos_y, sin_y], 1), precision=highest)
    first = jnp.dot(cos_x.T, summed, precision=highest)
    second = jnp.dot(sin_x.T, summed, precision=highest)
    real = first[:, :band] - second[:, band:]
    imag = -(second[:, :band] + first[:, band:])
    return (real, imag)


def column_block(cos_y, sin_y):
    upper = jnp.concatenate([cos_y.T, sin_y.T], 1)
    lower = jnp.concatenate([-sin_y.T, cos_y.T], 1)
    return jnp.concatenate([upper, lower], 0).astype(jnp.bfloat16)


def plane_intensity(kernel, weights, spec_re, spec_im, row_table, col_table):
    band = spec_re.shape[0]
    height = row_table.shape[0]
    width = col_table.shape[1] // 2

    def add_kernel(index, total):
        current = kernel[index].astype(jnp.float32)
        k_re = current[:, :band]
        k_im = current[:, band:]
        s_re = (k_re * spec_re - k_im * spec_im).astype(jnp.bfloat16)
        s_im = (k_re * spec_im + k_im * spec_re).astype(jnp.bfloat16)
        block = jnp.concatenate(
            [jnp.concatenate([s_re, s_im], 1), jnp.concatenate([-s_im, s_re], 1)], 0
        )
        half = jnp.dot(row_table, block, preferred_element_type=jnp.float32).astype(jnp.bfloat16)
        field = jnp.dot(half, col_table, preferred_element_type=jnp.float32)
        power = field[:, :width] * field[:, :width] + field[:, width:] * field[:, width:]
        return total + weights[index] * power

    return lax.fori_loop(0, kernel.shape[0], add_kernel, jnp.zeros((height, width), jnp.float32))


def extend(state, width):
    wide = padded(state, (("depth", 3), ("ty", 4)), width)
    lower = wide[:, :, :, :width]
    upper = wide[:, :, :, -width:]
    edges = padded(shortened(jnp.concatenate([upper, lower], 3)), (("tx", 3),), width)
    level = lax.axis_index("depth")
    last = lax.axis_size("depth") - 1
    lower = jnp.where(level == 0, edges[:, :, :, :width], lower)
    upper = jnp.where(level == last, edges[:, :, :, -width:], upper)
    return jnp.concatenate([lower, wide[:, :, :, width:-width], upper], 3)


def advance(wide):
    center = wide[:, :, :, 1:-1, 1:-1]
    lateral = (
        wide[:, :, :, 2:, 1:-1]
        + wide[:, :, :, :-2, 1:-1]
        + wide[:, :, :, 1:-1, 2:]
        + wide[:, :, :, 1:-1, :-2]
        - 4.0 * center
    )
    above = jnp.concatenate([center[:, 1:], center[:, -1:]], 1)
    below = jnp.concatenate([center[:, :1], center[:, :-1]], 1)
    vertical = above + below - 2.0 * center
    rate_lateral = jnp.array([0.23, 0.15], jnp.float32).reshape(2, 1, 1, 1, 1)
    rate_vertical = jnp.array([0.03, 0.05], jnp.float32).reshape(2, 1, 1, 1, 1)
    react = REACT_RATE * center[0] * center[1]
    return center + rate_lateral * lateral + rate_vertical * vertical - react[None]


def on_device(mask, kernels, weights, band_rows, band_cols, quencher):
    strip = mask.shape[1]
    tile = mask.shape[2]
    band = band_rows.shape[0]
    freq_x = band_rows - band // 2
    freq_y = band_cols - band // 2
    offset = lax.axis_index("depth") * strip
    cos_y, sin_y = phase_table(freq_y, tile, 0, tile)
    cos_x, sin_x = phase_table(freq_x, tile, offset, strip)
    part_re, part_im = mask_spectrum(mask[0].astype(jnp.float32), cos_x, sin_x, cos_y, sin_y)
    spec_re, spec_im = lax.psum((part_re, part_im), "depth")
    scale = 1.0 / (tile * tile)
    spec_re = spec_re * scale
    spec_im = spec_im * scale
    col_table = column_block(cos_y, sin_y)
    full_cos, full_sin = phase_table(freq_x, tile, 0, tile)
    row_table = jnp.concatenate([full_cos, full_sin], 1).astype(jnp.bfloat16)
    planes = [plane_intensity(kernels[0], weights, spec_re, spec_im, row_table, col_table)]
    intensity = lax.all_to_all(
        jnp.stack(planes, 0), "depth", split_axis=1, concat_axis=0, tiled=True
    )
    acid = 1.0 - jnp.exp(-DILL_RATE * intensity)
    state = jnp.stack([acid[:, None], quencher], 0)
    for turn in range(STEPS):
        state = advance(extend(state, 1))
    return (state[0], state[1])


def solution(mesh):
    placed = (
        P("tx", "depth", "ty"),
        P("depth", None, None, None),
        P(),
        P(),
        P(),
        P(None, "tx", "depth", "ty"),
    )
    return jax.shard_map(
        on_device,
        mesh=mesh,
        in_specs=placed,
        out_specs=(P(None, "tx", "depth", "ty"), P(None, "tx", "depth", "ty")),
        check_vma=False,
    )
```

profile of v0, /device:TPU:17, one launch (start us, length us, event | category | flops | bytes accessed | tf_op | source)
XLA Modules:
  0.0 243.1 jit_solution(7323824357931790094)
XLA Ops:
  7.0 29.3 %all-reduce = (f32[64,64]{1,0:T(8,128)S(1)}, f32[64,64]{1,0:T(8,128)S(1)}) all-reduce(f32[64,64]{1,0:T(8,128)S(1)} %get-tuple-element.226, f32[64,64]{1,0:T(8,128)S(1)} %get-tuple-element.225), channel_id=1, replica_groups=mesh['depth'=8,'tx'=8,'ty'=8] {'depth'}, use_global_device_ids=true, to_apply=%region_0.1 | all-reduce | flops 8192 | bytes 65536 | tf_op jit(solution)/shard_map/psum | solution.py:121
  37.7 82.6 %while.14 = (s32[]{:T(128)}, f32[512,512]{1,0:T(8,128)S(1)}, f32[12]{0:T(128)}, bf16[12,64,128]{2,1,0:T(8,128)(2,1)}, f32[64,64]{1,0:T(8,128)}, /*index=5*/f32[6...) while((s32[]{:T(128)}, f32[512,512]{1,0:T(8,128)S(1)}, ...), condition=%wide.region_3.4_spmd.clone, body=%wide.region_2.3_spmd.clone.sunk | while | flops 152809472 | bytes 6914187 | solution.py:78
  120.3 1.7 stack.9
  122.0 3.6 %all-to-all-start = ((f32[1,512,512]{2,0,1:T(1,128)}), f32[1,512,512]{2,0,1:T(1,128)S(1)}, u32[]{:S(2)}, u32[]{:S(2)}) async-start(f32[1,512,512]{2,0,1:T(1,128)} %stack.9), calls=%async_computation | async-start | bytes 2097152 | tf_op jit(solution)/shard_map/all_to_all | solution.py:129
  126.2 21.3 %all-to-all-done = f32[1,512,512]{2,0,1:T(1,128)S(1)} async-done(((f32[1,512,512]{2,0,1:T(1,128)}), f32[1,512,512]{2,0,1:T(1,128)S(1)}, u32[]{:S(2)}, u32[]{:S(2)}) %all-to-all-start) | async-done | bytes 1048608 | tf_op jit(solution)/shard_map/all_to_all | solution.py:129
  147.5 2.2 broadcast_multiply_fusion
  150.5 1.9 collective-permute-start
  152.4 4.6 %collective-permute-start.1 = (f32[2,8,1,1,512]{4,1,3,2,0:T(8,128)S(1)}, f32[2,8,1,1,512]{4,1,3,2,0:T(8,128)S(1)}, u32[]{:S(2)}, u32[]{:S(2)}) collective-permute-start(f32[2,8,1,1,512]{4,1,3,2,0:T(8,128)S(1)} %get-tuple-element.224), channel_id=1, source_target_pairs={{64,0},{128,64},{192,128},{256,192},{320,256},{384,320},{448,384},... | collective-permute-start | bytes 98312 | tf_op jit(solution)/shard_map/ppermute | solution.py:24
  157.0 2.5 %fusion.21 = (f32[2,7,1,64,512]{4,1,3,2,0:T(8,128)}, f32[2,7,1,64,512]{4,1,3,2,0:T(8,128)}) fusion(f32[1,8,1,64,512]{4,1,3,2,0:T(8,128)S(1)} %copy.20, f32[1,8,1,64,512]{4,1,3,2,0:T(8,128)S(1)} %bitcast.34), kind=kLoop, calls=%fused_computation.34 | loop fusion | flops 917504 | bytes 5767168 | tf_op jit(solution)/shard_map/stack | solution.py:133
  163.3 3.2 %collective-permute-start.2 = (f32[2,8,1,66,1]{3,1,4,2,0:T(8,128)S(1)}, f32[2,8,1,66,1]{3,1,4,2,0:T(8,128)S(1)}, u32[]{:S(2)}, u32[]{:S(2)}) collective-permute-start(f32[2,8,1,66,1]{3,1,4,2,0:T(8,128)S(1)} %copy.21), channel_id=1, source_target_pairs={{0,1},{1,2},{2,3},{3,4},{4,5},{5,6},{6,7},{7,0},{8,9},{9,10},{10,1... | collective-permute-start | bytes 12680 | tf_op jit(solution)/shard_map/ppermute | solution.py:22
  166.5 4.2 %collective-permute-start.3 = (f32[2,8,1,66,1]{3,1,4,2,0:T(8,128)S(1)}, f32[2,8,1,66,1]{3,1,4,2,0:T(8,128)S(1)}, u32[]{:S(2)}, u32[]{:S(2)}) collective-permute-start(f32[2,8,1,66,1]{3,1,4,2,0:T(8,128)S(1)} %copy.22), channel_id=1, source_target_pairs={{1,0},{2,1},{3,2},{4,3},{5,4},{6,5},{7,6},{0,7},{9,8},{10,9},{11,1... | collective-permute-start | bytes 12680 | tf_op jit(solution)/shard_map/ppermute | solution.py:24
  171.7 1.6 copy.28
  174.1 10.9 %collective-permute-start.4 = (bf16[2,8,1,1,514]{4,1,3,2,0:T(8,128)(2,1)S(1)}, bf16[2,8,1,1,514]{4,1,3,2,0:T(8,128)(2,1)S(1)}, u32[]{:S(2)}, u32[]{:S(2)}) collective-permute-start(bf16[2,8,1,1,514]{4,1,3,2,0:T(8,128)(2,1)S(1)} %get-tuple-element.199), channel_id=1, source_target_pairs={{8,0},{16,8},{24,16},{32,24},{40,32},{48,40},{56,48},{0,56},{9,1},... | collective-permute-start | bytes 49352 | tf_op jit(solution)/shard_map/ppermute | solution.py:24
  185.0 5.3 %collective-permute-start.5 = (bf16[2,8,1,1,514]{4,1,3,2,0:T(8,128)(2,1)S(1)}, bf16[2,8,1,1,514]{4,1,3,2,0:T(8,128)(2,1)S(1)}, u32[]{:S(2)}, u32[]{:S(2)}) collective-permute-start(bf16[2,8,1,1,514]{4,1,3,2,0:T(8,128)(2,1)S(1)} %get-tuple-element.205), channel_id=1, source_target_pairs={{0,8},{8,16},{16,24},{24,32},{32,40},{40,48},{48,56},{56,0},{1,9},... | collective-permute-start | bytes 49352 | tf_op jit(solution)/shard_map/ppermute | solution.py:22
  193.9 6.3 %fusion.35 = f32[2,8,1,64,512]{4,1,3,2,0:T(8,128)S(1)} fusion(f32[2,8,1,66,1]{4,1,3,2,0:T(8,128)} %copy-done.4, f32[2,8,1,1,512]{4,1,3,2,0:T(8,128)S(1)} %collective-permute-done.1, f32[2,8,1,1,512]{4,1,3,2,0:T(8,128)S(1)} %collective-permute-done, f32[1,8,1,64,512]{4,1,3,2,0:T(8,128)S(1)} %bitcast.39, f32[1,8,1,64,512]{4,1,3,2,0:T(8,128)S(1)} %copy-done.1, ...), kind=kLoop, calls=%fused_computation.57 | loop fusion | flops 13631488 | bytes 11682320 | tf_op jit(solution)/shard_map/sub | solution.py:108
  200.2 2.6 %fusion.102 = (f32[2,7,1,64,512]{4,1,3,2,0:T(8,128)}, f32[2,7,1,64,512]{4,1,3,2,0:T(8,128)}) fusion(f32[2,8,1,64,512]{4,1,3,2,0:T(8,128)S(1)} %fusion.35), kind=kLoop, calls=%fused_computation.183 | loop fusion | bytes 7340032 | tf_op jit(solution)/shard_map/slice | solution.py:103
  202.9 1.9 collective-permute-start.6
  204.8 4.6 %collective-permute-start.7 = (f32[2,8,1,1,512]{4,1,3,2,0:T(8,128)S(1)}, f32[2,8,1,1,512]{4,1,3,2,0:T(8,128)S(1)}, u32[]{:S(2)}, u32[]{:S(2)}) collective-permute-start(f32[2,8,1,1,512]{4,1,3,2,0:T(8,128)S(1)} %get-tuple-element.218), channel_id=1, source_target_pairs={{64,0},{128,64},{192,128},{256,192},{320,256},{384,320},{448,384},... | collective-permute-start | bytes 98312 | tf_op jit(solution)/shard_map/ppermute | solution.py:24
  212.9 2.4 collective-permute-start.8
  215.3 5.0 %collective-permute-start.9 = (f32[2,8,1,66,1]{3,1,4,2,0:T(8,128)S(1)}, f32[2,8,1,66,1]{3,1,4,2,0:T(8,128)S(1)}, u32[]{:S(2)}, u32[]{:S(2)}) collective-permute-start(f32[2,8,1,66,1]{3,1,4,2,0:T(8,128)S(1)} %copy.30), channel_id=1, source_target_pairs={{1,0},{2,1},{3,2},{4,3},{5,4},{6,5},{7,6},{0,7},{9,8},{10,9},{11,1... | collective-permute-start | bytes 12680 | tf_op jit(solution)/shard_map/ppermute | solution.py:24
  223.8 1.9 collective-permute-start.10
  225.7 5.8 %collective-permute-start.11 = (bf16[2,8,1,1,514]{4,1,3,2,0:T(8,128)(2,1)S(1)}, bf16[2,8,1,1,514]{4,1,3,2,0:T(8,128)(2,1)S(1)}, u32[]{:S(2)}, u32[]{:S(2)}) collective-permute-start(bf16[2,8,1,1,514]{4,1,3,2,0:T(8,128)(2,1)S(1)} %get-tuple-element.203), channel_id=1, source_target_pairs={{0,8},{8,16},{16,24},{24,32},{32,40},{40,48},{48,56},{56,0},{1,9},... | collective-permute-start | bytes 49352 | tf_op jit(solution)/shard_map/ppermute | solution.py:22
  234.9 4.8 %fusion.27 = f32[2,8,1,64,512]{4,1,3,2,0:T(8,128)S(1)} fusion(f32[2,8,1,64,512]{4,1,3,2,0:T(8,128)S(1)} %fusion.35, f32[2,8,1,66,1]{4,1,3,2,0:T(8,128)S(1)} %copy-done.3, f32[2,8,1,1,512]{4,1,3,2,0:T(8,128)S(1)} %collective-permute-done.7, f32[2,8,1,1,512]{4,1,3,2,0:T(8,128)S(1)} %collective-permute-done.6, f32[2,8,1,66,1]{4,1,3,2,0:T(8,128)S(1)} %copy.32, ...), kind=kLoop, calls=%fused_computation.41 | loop fusion | flops 12058624 | bytes 11682320 | tf_op jit(solution)/shard_map/sub | solution.py:108
  239.9 1.6 copy.36
  (158 shorter events, 112.4 us)
Async XLA Ops:
  120.2 5.3 %copy-start.9 = (f32[8,1,64,512]{3,2,1,0:T(8,128)S(1)}, f32[8,1,64,512]{3,2,1,0:T(8,128)}, u32[]{:S(2)}) copy-start(f32[8,1,64,512]{3,2,1,0:T(8,128)} %param.17) | copy-start | bytes 3145732
  122.0 25.5 %all-to-all-start = ((f32[1,512,512]{2,0,1:T(1,128)}), f32[1,512,512]{2,0,1:T(1,128)S(1)}, u32[]{:S(2)}, u32[]{:S(2)}) async-start(f32[1,512,512]{2,0,1:T(1,128)} %stack.9), calls=%async_computation | async-start | bytes 2097152 | tf_op jit(solution)/shard_map/all_to_all | solution.py:129
  150.5 39.9 %copy-start = (f32[1,8,1,64,512]{4,1,3,2,0:T(8,128)}, f32[1,8,1,64,512]{4,1,3,2,0:T(8,128)S(1)}, u32[]{:S(2)}) copy-start(f32[1,8,1,64,512]{4,1,3,2,0:T(8,128)S(1)} %copy.20) | copy-start | bytes 3145732
  150.5 9.1 %collective-permute-start = (f32[2,8,1,1,512]{4,1,3,2,0:T(8,128)S(1)}, f32[2,8,1,1,512]{4,1,3,2,0:T(8,128)S(1)}, u32[]{:S(2)}, u32[]{:S(2)}) collective-permute-start(f32[2,8,1,1,512]{4,1,3,2,0:T(8,128)S(1)} %get-tuple-element.223), channel_id=1, source_target_pairs={{0,64},{64,128},{128,192},{192,256},{256,320},{320,384},{384,448},... | collective-permute-start | bytes 98312 | tf_op jit(solution)/shard_map/ppermute | solution.py:22
  152.4 7.1 %collective-permute-start.1 = (f32[2,8,1,1,512]{4,1,3,2,0:T(8,128)S(1)}, f32[2,8,1,1,512]{4,1,3,2,0:T(8,128)S(1)}, u32[]{:S(2)}, u32[]{:S(2)}) collective-permute-start(f32[2,8,1,1,512]{4,1,3,2,0:T(8,128)S(1)} %get-tuple-element.224), channel_id=1, source_target_pairs={{64,0},{128,64},{192,128},{256,192},{320,256},{384,320},{448,384},... | collective-permute-start | bytes 98312 | tf_op jit(solution)/shard_map/ppermute | solution.py:24
  163.3 10.4 %collective-permute-start.2 = (f32[2,8,1,66,1]{3,1,4,2,0:T(8,128)S(1)}, f32[2,8,1,66,1]{3,1,4,2,0:T(8,128)S(1)}, u32[]{:S(2)}, u32[]{:S(2)}) collective-permute-start(f32[2,8,1,66,1]{3,1,4,2,0:T(8,128)S(1)} %copy.21), channel_id=1, source_target_pairs={{0,1},{1,2},{2,3},{3,4},{4,5},{5,6},{6,7},{7,0},{8,9},{9,10},{10,1... | collective-permute-start | bytes 12680 | tf_op jit(solution)/shard_map/ppermute | solution.py:22
  166.5 6.8 %collective-permute-start.3 = (f32[2,8,1,66,1]{3,1,4,2,0:T(8,128)S(1)}, f32[2,8,1,66,1]{3,1,4,2,0:T(8,128)S(1)}, u32[]{:S(2)}, u32[]{:S(2)}) collective-permute-start(f32[2,8,1,66,1]{3,1,4,2,0:T(8,128)S(1)} %copy.22), channel_id=1, source_target_pairs={{1,0},{2,1},{3,2},{4,3},{5,4},{6,5},{7,6},{0,7},{9,8},{10,9},{11,1... | collective-permute-start | bytes 12680 | tf_op jit(solution)/shard_map/ppermute | solution.py:24
  173.6 17.6 %copy-start.2 = (f32[2,8,1,66,1]{4,1,3,2,0:T(8,128)}, f32[2,8,1,66,1]{4,1,3,2,0:T(8,128)S(1)}, u32[]{:S(2)}) copy-start(f32[2,8,1,66,1]{4,1,3,2,0:T(8,128)S(1)} %copy.24) | copy-start | bytes 12676
  174.0 17.3 %copy-start.4 = (f32[2,8,1,66,1]{4,1,3,2,0:T(8,128)}, f32[2,8,1,66,1]{4,1,3,2,0:T(8,128)S(1)}, u32[]{:S(2)}) copy-start(f32[2,8,1,66,1]{4,1,3,2,0:T(8,128)S(1)} %copy.23) | copy-start | bytes 12676
  174.1 17.5 %collective-permute-start.4 = (bf16[2,8,1,1,514]{4,1,3,2,0:T(8,128)(2,1)S(1)}, bf16[2,8,1,1,514]{4,1,3,2,0:T(8,128)(2,1)S(1)}, u32[]{:S(2)}, u32[]{:S(2)}) collective-permute-start(bf16[2,8,1,1,514]{4,1,3,2,0:T(8,128)(2,1)S(1)} %get-tuple-element.199), channel_id=1, source_target_pairs={{8,0},{16,8},{24,16},{32,24},{40,32},{48,40},{56,48},{0,56},{9,1},... | collective-permute-start | bytes 49352 | tf_op jit(solution)/shard_map/ppermute | solution.py:24
  185.0 6.6 %collective-permute-start.5 = (bf16[2,8,1,1,514]{4,1,3,2,0:T(8,128)(2,1)S(1)}, bf16[2,8,1,1,514]{4,1,3,2,0:T(8,128)(2,1)S(1)}, u32[]{:S(2)}, u32[]{:S(2)}) collective-permute-start(bf16[2,8,1,1,514]{4,1,3,2,0:T(8,128)(2,1)S(1)} %get-tuple-element.205), channel_id=1, source_target_pairs={{0,8},{8,16},{16,24},{24,32},{32,40},{40,48},{48,56},{56,0},{1,9},... | collective-permute-start | bytes 49352 | tf_op jit(solution)/shard_map/ppermute | solution.py:22
  191.3 2.0 copy-start.5
  191.3 2.6 %copy-start.6 = (f32[2,7,1,64,512]{4,1,3,2,0:T(8,128)S(1)}, f32[2,7,1,64,512]{4,1,3,2,0:T(8,128)}, u32[]{:S(2)}) copy-start(f32[2,7,1,64,512]{4,1,3,2,0:T(8,128)} %get-tuple-element.222) | copy-start | bytes 5505028
  191.3 2.6 %copy-start.13 = (f32[2]{0:T(128)S(1)}, f32[2]{0:T(128)}, u32[]{:S(2)}) copy-start(f32[2]{0:T(128)} %constant.89.clone) | copy-start | bytes 28
  191.3 2.6 %copy-start.14 = (f32[2]{0:T(128)S(1)}, f32[2]{0:T(128)}, u32[]{:S(2)}) copy-start(f32[2]{0:T(128)} %constant.88.clone) | copy-start | bytes 28
  202.9 6.8 %collective-permute-start.6 = (f32[2,8,1,1,512]{4,1,3,2,0:T(8,128)S(1)}, f32[2,8,1,1,512]{4,1,3,2,0:T(8,128)S(1)}, u32[]{:S(2)}, u32[]{:S(2)}) collective-permute-start(f32[2,8,1,1,512]{4,1,3,2,0:T(8,128)S(1)} %get-tuple-element.217), channel_id=1, source_target_pairs={{0,64},{64,128},{128,192},{192,256},{256,320},{320,384},{384,448},... | collective-permute-start | bytes 98312 | tf_op jit(solution)/shard_map/ppermute | solution.py:22
  204.8 5.6 %collective-permute-start.7 = (f32[2,8,1,1,512]{4,1,3,2,0:T(8,128)S(1)}, f32[2,8,1,1,512]{4,1,3,2,0:T(8,128)S(1)}, u32[]{:S(2)}, u32[]{:S(2)}) collective-permute-start(f32[2,8,1,1,512]{4,1,3,2,0:T(8,128)S(1)} %get-tuple-element.218), channel_id=1, source_target_pairs={{64,0},{128,64},{192,128},{256,192},{320,256},{384,320},{448,384},... | collective-permute-start | bytes 98312 | tf_op jit(solution)/shard_map/ppermute | solution.py:24
  212.9 8.9 %collective-permute-start.8 = (f32[2,8,1,66,1]{3,1,4,2,0:T(8,128)S(1)}, f32[2,8,1,66,1]{3,1,4,2,0:T(8,128)S(1)}, u32[]{:S(2)}, u32[]{:S(2)}) collective-permute-start(f32[2,8,1,66,1]{3,1,4,2,0:T(8,128)S(1)} %copy.29), channel_id=1, source_target_pairs={{0,1},{1,2},{2,3},{3,4},{4,5},{5,6},{6,7},{7,0},{8,9},{9,10},{10,1... | collective-permute-start | bytes 12680 | tf_op jit(solution)/shard_map/ppermute | solution.py:22
  215.3 6.2 %collective-permute-start.9 = (f32[2,8,1,66,1]{3,1,4,2,0:T(8,128)S(1)}, f32[2,8,1,66,1]{3,1,4,2,0:T(8,128)S(1)}, u32[]{:S(2)}, u32[]{:S(2)}) collective-permute-start(f32[2,8,1,66,1]{3,1,4,2,0:T(8,128)S(1)} %copy.30), channel_id=1, source_target_pairs={{1,0},{2,1},{3,2},{4,3},{5,4},{6,5},{7,6},{0,7},{9,8},{10,9},{11,1... | collective-permute-start | bytes 12680 | tf_op jit(solution)/shard_map/ppermute | solution.py:24
  222.9 8.6 %copy-start.3 = (f32[2,8,1,66,1]{4,1,3,2,0:T(8,128)S(1)}, f32[2,8,1,66,1]{4,1,3,2,0:T(8,128)}, u32[]{:S(2)}) copy-start(f32[2,8,1,66,1]{4,1,3,2,0:T(8,128)} %copy.31) | copy-start | bytes 12676
  223.8 8.8 %collective-permute-start.10 = (bf16[2,8,1,1,514]{4,1,3,2,0:T(8,128)(2,1)S(1)}, bf16[2,8,1,1,514]{4,1,3,2,0:T(8,128)(2,1)S(1)}, u32[]{:S(2)}, u32[]{:S(2)}) collective-permute-start(bf16[2,8,1,1,514]{4,1,3,2,0:T(8,128)(2,1)S(1)} %get-tuple-element.193), channel_id=1, source_target_pairs={{8,0},{16,8},{24,16},{32,24},{40,32},{48,40},{56,48},{0,56},{9,1},... | collective-permute-start | bytes 49352 | tf_op jit(solution)/shard_map/ppermute | solution.py:24
  225.7 6.9 %collective-permute-start.11 = (bf16[2,8,1,1,514]{4,1,3,2,0:T(8,128)(2,1)S(1)}, bf16[2,8,1,1,514]{4,1,3,2,0:T(8,128)(2,1)S(1)}, u32[]{:S(2)}, u32[]{:S(2)}) collective-permute-start(bf16[2,8,1,1,514]{4,1,3,2,0:T(8,128)(2,1)S(1)} %get-tuple-element.203), channel_id=1, source_target_pairs={{0,8},{8,16},{16,24},{24,32},{32,40},{40,48},{48,56},{56,0},{1,9},... | collective-permute-start | bytes 49352 | tf_op jit(solution)/shard_map/ppermute | solution.py:22
  232.4 2.2 copy-start.8
  232.4 2.5 %copy-start.10 = (f32[8,64,512]{2,0,1:T(8,128)S(1)}, f32[8,64,512]{2,0,1:T(8,128)}, u32[]{:S(2)}) copy-start(f32[8,64,512]{2,0,1:T(8,128)} %fusion.43) | copy-start | bytes 3145732
  (4 other events, 5.4 us)
where the time goes:
time: 248 us; the launch traced here: 243 us
  other arithmetic  79 us (32%)
  starting transfers between devices  55.2 us (22%)
  local copies, waits for them, and re-layouts  36.5 us (15%)
  blocking collectives  29.3 us (12%)
  waiting for transfers between devices  22 us (9%)
  matrix products  19.6 us (8%)
    ppermute x6, starting transfers between devices, padded(): lax.ppermute(head, axis, [((i + 1) % count, i) for i in range(count)])  31.2 us
    psum x1, blocking collectives, on_device(): spec_re, spec_im = lax.psum((part_re, part_im), 'depth')  29.3 us
    all_to_all x1, waiting for transfers between devices, on_device(): lax.all_to_all(jnp.stack(planes, 0), 'depth', split_axis=1, concat_axis=0...  21.3 us
    ppermute x6, starting transfers between devices, padded(): lax.ppermute(tail, axis, [(i, (i + 1) % count) for i in range(count)])  20.5 us
    neg x12, other arithmetic, add_kernel(): -s_im  17.6 us
    dot_general x12, matrix products, add_kernel(): field = jnp.dot(half, col_table, preferred_element_type=jnp.float32)  17.4 us
    dynamic_slice x12, local copies, waits for them, and re-layouts, add_kernel(): return total + weights[index] * power  14.6 us
    add x12, other arithmetic, add_kernel(): return total + weights[index] * power  13.8 us
  transfers between devices with their start and end apart: 13, of which 2 were waited for; matrix products, arithmetic and copies ran while one was open for 4% of the time, Pallas kernels for 0%

commit v1 on v0

v1 whole, which is shorter than its diff:
```python
import functools
import math

import jax
import jax.numpy as jnp
import numpy as np
from jax import lax
from jax.experimental import pallas as pl
from jax.experimental.pallas import tpu as pltpu
from jax.sharding import PartitionSpec as P

BF = jnp.bfloat16
F32 = jnp.float32
TILE = 512
BAND = 64
HALF = 256
PLANES = 8
STRIP = 64
CYC = 72
WIDE = 640
DILL_RATE = 1.0
REACT_RATE = 0.4
ACID_LAT, ACID_VERT = 0.23, 0.03
QUEN_LAT, QUEN_VERT = 0.15, 0.05
VMEM = pl.BlockSpec(memory_space=pltpu.VMEM)
SMEM = pl.BlockSpec(memory_space=pltpu.SMEM)
LIMIT = 40 * 1024 * 1024
MOST = 60 * 1024 * 1024


def split(x):
    hi = np.asarray(x, np.float32).astype(jnp.bfloat16)
    lo = (np.asarray(x, np.float64) - hi.astype(np.float64)).astype(np.float32).astype(jnp.bfloat16)
    return hi, lo


@functools.cache
def constants():
    u = np.arange(TILE)
    f = np.arange(128) - BAND // 2
    angle = np.mod(u[:, None] * f[None, :], TILE) * (2.0 * np.pi / TILE)
    cs = np.concatenate([np.cos(angle), np.sin(angle)], 1)
    n = np.arange(HALF)
    m = np.arange(1, 128)
    gap = np.mod(u[None, :] - 2 * n[:, None], TILE)
    line = (1.0 + 2.0 * np.cos(2.0 * np.pi * m[None, :] * u[:, None] / TILE).sum(1)) / HALF
    spread = line[gap]
    spread[:, 0::2] = np.eye(HALF)
    out = {}
    out["cs"] = split(cs)[0]
    out["pairs_hi"], out["pairs_lo"] = split(cs[0::2] + cs[1::2])
    out["even_t"] = split(cs[0::2].T)[0]
    edge = np.zeros((16, 256))
    edge[:4] = cs[[0, 1, TILE - 2, TILE - 1]]
    out["edge"] = split(edge)[0]
    out["spread"] = np.concatenate(split(spread), 0)
    return out


def dot(a, b):
    return lax.dot_general(a, b, (((1,), (0,)), ((), ())), preferred_element_type=F32)


def dot_nt(a, b):
    return lax.dot_general(a, b, (((1,), (1,)), ((), ())), preferred_element_type=F32)


def dot_tn(a, b):
    return lax.dot_general(a, b, (((0,), (0,)), ((), ())), preferred_element_type=F32)


def iota(shape, dim):
    return lax.broadcasted_iota(jnp.int32, shape, dim)


def fetch(sem, *pairs):
    copies = [pltpu.make_async_copy(src, dst, sem.at[i]) for i, (src, dst) in enumerate(pairs)]
    for copy in copies:
        copy.start()
    return copies


def picker(band_ref):
    band = band_ref[...]
    return (iota((256, 128), 0) == jnp.concatenate([band, band + 128], 1)).astype(BF)


def columns():
    row = iota((16, TILE), 0)
    col = jnp.where(row < 2, row, row + TILE - 4)
    return ((iota((16, TILE), 1) == col) & (row < 4)).astype(BF)


def strip_kernel(mask_in, quen_in, out_ref, mask, head, tail, edge, sem):
    copies = fetch(
        sem, *[(mask_in.at[:, pl.ds(128 * c, 128)], mask.at[c]) for c in range(4)],
        (quen_in.at[:, pl.ds(0, 8), :], head), (quen_in.at[:, pl.ds(STRIP - 8, 8), :], tail),
    )
    halves = (iota((TILE, HALF), 0) == 2 * iota((TILE, HALF), 1)).astype(BF)
    before = lax.rem(lax.axis_index("depth") + 7, 8)
    for copy in copies[:4]:
        copy.wait()
    rows = [mask[c, pl.ds(0, STRIP // 2, stride=2), :] for c in range(4)]
    coarse = dot(jnp.concatenate(rows, 1).astype(F32).astype(BF), halves).astype(BF)
    for copy in copies[4:]:
        copy.wait()
    for z in range(PLANES):
        for r in range(2):
            edge[8 * r + z : 8 * r + z + 1, :] = head[z, r : r + 1, :]
            edge[16 + 8 * r + z : 17 + 8 * r + z, :] = tail[z, 6 + r : 7 + r, :]
    top = edge[0:16].astype(BF)
    bottom = edge[16:32].astype(BF)
    for peer in range(8):
        out_ref[peer, 0:32, :] = coarse[:, 0:128]
        out_ref[peer, 32:64, :] = coarse[:, 128:256]
        ours = jnp.where(before == peer, top, bottom)
        for c in range(4):
            out_ref[peer, 64 + 16 * c : 80 + 16 * c, :] = ours[:, 128 * c : 128 * (c + 1)]


def table_kernel(
    after, bx_in, by_in, cs_in, hi_in, lo_in, even_in, edge_in, quen_in, w_in,
    rows_ref, xhi_ref, xlo_ref, yhi_ref, ylo_ref, cols_ref, placed_ref, side_ref, weight_ref,
    bx, by, cs, hi_tab, lo_tab, even, edge, quen, w, sem,
):
    copies = fetch(
        sem, (bx_in, bx), (by_in, by), (edge_in, edge), (even_in, even), (cs_in, cs), (hi_in, hi_tab), (lo_in, lo_tab),
        (w_in, w), (quen_in, quen),
    )
    for copy in copies[:8]:
        copy.wait()
    pick_x = picker(bx)
    pick_y = picker(by)
    rows_ref[...] = dot(cs[...], pick_x).astype(BF)
    xhi_ref[...] = dot(hi_tab[...], pick_x).astype(BF)
    xlo_ref[...] = dot(lo_tab[...], pick_x).astype(BF)
    yhi_ref[...] = dot(hi_tab[...], pick_y).astype(BF)
    ylo_ref[...] = dot(lo_tab[...], pick_y).astype(BF)
    table = dot_tn(pick_y, even[...])
    flip = jnp.where(iota((128, 1), 0) < BAND, 1.0, -1.0).astype(F32)
    cols_ref[:, 0:HALF] = (table * flip).astype(BF)
    cols_ref[:, HALF:TILE] = jnp.concatenate([table[BAND:], table[:BAND]], 0).astype(BF)
    sign = jnp.where(iota((1, 128), 1) < BAND, 1.0, -1.0).astype(F32)
    ends = dot(edge[...], pick_y)[0:8]
    ends = jnp.where(iota((8, 128), 0) < 4, sign * ends, pltpu.roll(pltpu.roll(ends, BAND, 1), 4, 0))
    count = placed_ref.shape[1] // 128
    own = iota((128, 128), 0) >> 3
    many = jnp.tile(ends, (16, 1))
    for k in range(count):
        placed_ref[:, 128 * k : 128 * (k + 1)] = jnp.where(own == k, many, 0.0).astype(BF)
        weight_ref[k : k + 1, :] = jnp.full((1, HALF), w[k], F32)
    copies[8].wait()
    pick = columns()
    for z in range(PLANES):
        side_ref[z] = dot_nt(pick, quen[z].astype(BF))


def spectrum_kernel(
    w_ref, got_ref, kern_ref, rows_ref, xhi_ref, xlo_ref, yhi_ref, ylo_ref, placed_ref, side_ref,
    big_ref, left_ref, right_ref, ring_ref,
):
    lane = iota((1, 128), 1)
    sign = jnp.where(lane < BAND, -1.0, 1.0).astype(F32)
    coarse = jnp.concatenate([got_ref[:, 0:32, :].reshape(256, 128), got_ref[:, 32:64, :].reshape(256, 128)], 1)
    summed = dot(coarse, yhi_ref[...]) + dot(coarse, ylo_ref[...])
    hi = summed.astype(BF)
    lo = (summed - hi.astype(F32)).astype(BF)
    u = (dot_tn(xhi_ref[...], hi) + dot_tn(xhi_ref[...], lo) + dot_tn(xlo_ref[...], hi)) * (1.0 / (TILE * TILE))
    v = u[:BAND] + sign * pltpu.roll(u[BAND:], BAND, 1)
    v_swap = pltpu.roll(v, BAND, 1)
    coef_a = jnp.where(lane < BAND, v, v_swap)
    coef_b = jnp.where(lane < BAND, v_swap, -v)
    count = kern_ref.shape[0]
    for k in range(count):
        cur = kern_ref[k].astype(F32)
        top = cur * coef_a + pltpu.roll(cur, BAND, 1) * coef_b
        big_ref[0:BAND, 128 * k : 128 * (k + 1)] = top.astype(BF)
        big_ref[BAND:128, 128 * k : 128 * (k + 1)] = (sign * pltpu.roll(top, BAND, 1)).astype(BF)
    narrow = dot_nt(placed_ref[...], big_ref[...]).astype(BF)
    field = dot_nt(narrow, rows_ref[...])
    total = jnp.zeros((8, TILE), F32)
    for k in range(count):
        part = field[8 * k : 8 * (k + 1)]
        total = total + w_ref[k : k + 1, 0:1] * (part * part)
    bright = total + pltpu.roll(total, 4, 0)
    place = iota((16, TILE), 0)
    eight = jnp.concatenate([bright, bright], 0)
    left_ref[0:16, :] = jnp.where(place < 2, eight, 0.0).astype(BF)
    right_ref[0:16, :] = jnp.where(place < 2, pltpu.roll(eight, 14, 0), 0.0).astype(BF)
    me = lax.axis_index("depth")
    before = lax.rem(me + 7, 8)
    after = lax.rem(me + 1, 8)
    for c in range(4):
        low = got_ref[after, 64 + 16 * c : 80 + 16 * c, :].astype(F32)
        high = got_ref[before, 64 + 16 * c : 80 + 16 * c, :].astype(F32)
        for z in range(PLANES):
            ring_ref[z, 2:6, 128 * c : 128 * (c + 1)] = jnp.zeros((4, 128), F32)
            for r in range(2):
                spot = 8 * r + z
                ring_ref[z, r : r + 1, 128 * c : 128 * (c + 1)] = low[spot : spot + 1]
                ring_ref[z, 6 + r : 7 + r, 128 * c : 128 * (c + 1)] = high[spot : spot + 1]
    left_ref[16:32, :] = jnp.zeros((16, TILE), BF)
    right_ref[16:32, :] = jnp.zeros((16, TILE), BF)
    ring = dot_nt(columns(), ring_ref[...].reshape(PLANES * 8, TILE).astype(BF))
    lefts, rights = [], []
    for z in range(PLANES):
        cols = jnp.concatenate([side_ref[z], ring if z == 0 else pltpu.roll(ring, STRIP - 8 * z, 1)], 1)
        lefts.append(cols[0:2])
        rights.append(cols[2:4])
    left_ref[16:32, 0:128] = jnp.concatenate(lefts, 0).astype(BF)
    right_ref[16:32, 0:128] = jnp.concatenate(rights, 0).astype(BF)


def image_kernel(w_ref, big_ref, rows_ref, cols_ref, img_ref):
    count = big_ref.shape[1] // 128
    chunk = 128
    cols = cols_ref[...]
    for part in range(TILE // chunk):
        half = dot(rows_ref[part * chunk : (part + 1) * chunk, :], big_ref[...]).astype(BF)
        total = jnp.zeros((chunk, HALF), F32)
        for k in range(count):
            field = dot(half[:, 128 * k : 128 * (k + 1)], cols)
            total = total + w_ref[k : k + 1, :] * (field[:, :HALF] * field[:, :HALF] + field[:, HALF:] * field[:, HALF:])
        img_ref[part * chunk : (part + 1) * chunk, :] = total


def pack_kernel(img_ref, from_left, from_right, out_ref, scr_ref):
    place = iota((8, TILE), 0)
    both = jnp.where(place < 2, from_left[0:16, :].astype(F32)[0:8], pltpu.roll(from_right[0:16, :].astype(F32)[0:8], 2, 0))
    lane = iota((8, HALF), 1)
    scr_ref[...] = jnp.zeros((16, HALF), F32)
    for p in range(8):
        base = p * STRIP
        out_ref[p, 0:STRIP, :] = img_ref[base : base + STRIP, :].astype(BF)
        nxt = (base + STRIP) % TILE
        scr_ref[0:2, :] = img_ref[nxt : nxt + 2, :]
        prv = (base - 2) % TILE
        scr_ref[6:8, :] = img_ref[prv : prv + 2, :]
        first = pltpu.roll(both, (TILE - base) % TILE, 1)[:, :HALF]
        second = pltpu.roll(both, (TILE - base + CYC) % TILE, 1)[:, :HALF]
        side = jnp.where(lane < 66, first, jnp.where(lane < CYC, second, 0.0))
        scr_ref[2:6, :] = side[0:4]
        out_ref[p, STRIP:80, :] = scr_ref[...].astype(BF)


def planes_side(source, spots):
    count = source.shape[0]
    row = iota((count, 128 * PLANES), 0)
    col = iota((count, 128 * PLANES), 1)
    z, lane = col >> 7, col & 127
    hit = row < 0
    for spot, place in zip(spots, (126, 127, 0, 1)):
        hit = hit | ((row == spot(z)) & (lane == place))
    return dot_tn(source, hit.astype(BF))


def acid_side(got_ref):
    tails = got_ref[:, 64:80, 0:128].reshape(16 * PLANES, 128)
    return planes_side(tails, [lambda z, j=j: 16 * z + 2 + j for j in range(4)])


def quen_side(from_left, from_right):
    both = jnp.concatenate([from_left[16:32, 0:128], from_right[16:32, 0:128]], 0)
    return planes_side(both, [lambda z, j=j: 2 * z + j for j in (0, 1, 16, 17)])


def exposed(intensity):
    return 1.0 - jnp.exp(-DILL_RATE * intensity)


def edge_kernel(got_ref, spread_ref, quen_in, from_left, from_right, tile_ref, m_ref, near, far, scr, sem):
    copies = fetch(sem, (quen_in.at[:, pl.ds(0, 8), :], near), (quen_in.at[:, pl.ds(STRIP - 8, 8), :], far))
    last = lax.axis_index("depth") == 7
    start = pl.multiple_of(jnp.where(last, STRIP - 16, 0), 16)
    coarse = jnp.concatenate([got_ref[z, pl.ds(start, 16), :] for z in range(PLANES)], 0)
    fine = exposed(dot(jnp.concatenate([coarse, coarse], 1), spread_ref[...]))
    side = acid_side(got_ref)
    side = exposed(jnp.where(last, side[STRIP - 8 : STRIP], side[0:8]))
    side_q = quen_side(from_left, from_right)
    side_q = jnp.where(last, side_q[STRIP - 8 : STRIP], side_q[0:8])
    for copy in copies:
        copy.wait()
    for z in range(PLANES):
        mine = fine[16 * z : 16 * (z + 1)]
        tile_ref[0, z, :, 0:TILE] = jnp.where(last, mine[8:16], mine[0:8])
        tile_ref[0, z, :, TILE:WIDE] = side[:, 128 * z : 128 * (z + 1)]
        tile_ref[1, z, :, 0:TILE] = jnp.where(last, far[z], near[z])
        tile_ref[1, z, :, TILE:WIDE] = side_q[:, 128 * z : 128 * (z + 1)]
    for f in range(2):
        for z in range(PLANES):
            outer = jnp.where(last, tile_ref[f, z, 6:8, :], tile_ref[f, z, 0:2, :])
            scr[16 * f + 2 * z : 16 * f + 2 * z + 2, :] = outer
    m_ref[...] = scr[...].astype(BF)


def moved(src_a, src_q, z, rows, cols):
    height, width = src_a.shape[1:]
    a = src_a[z, 0:rows, 0:cols]
    q = src_q[z, 0:rows, 0:cols]
    react = REACT_RATE * a * q

    def move(c, ref, lat, vert):
        up = ref[min(z + 1, PLANES - 1), 0:rows, 0:cols]
        down = ref[max(z - 1, 0), 0:rows, 0:cols]
        tall = ref[z, :, 0:cols]
        wide = ref[z, 0:rows, :]
        near = (pltpu.roll(tall, 1, 0) + pltpu.roll(tall, height - 1, 0))[0:rows]
        near = near + (pltpu.roll(wide, 1, 1)[:, 0:cols] + pltpu.roll(wide, width - 1, 1)[:, 0:cols])
        return (1.0 - 4.0 * lat - 2.0 * vert) * c + lat * near + vert * (up + down) - react

    return move(a, src_a, ACID_LAT, ACID_VERT), move(q, src_q, QUEN_LAT, QUEN_VERT)


def bake_kernel(
    got_ref, spread_ref, quen_in, ring_ref, from_left, from_right, a_out, q_out,
    a_ref, q_ref, a_mid, q_mid, a_end, q_end, sem,
):
    copy = pltpu.make_async_copy(quen_in, q_ref.at[:, pl.ds(0, STRIP), pl.ds(0, TILE)], sem.at[0, 0])
    copy.start()
    side = exposed(acid_side(got_ref))
    side_q = quen_side(from_left, from_right)
    coarse = got_ref[...].reshape(PLANES * 80, HALF)
    fine = dot(jnp.concatenate([coarse, coarse], 1), spread_ref[...])
    for z in range(PLANES):
        a_ref[z, :, 0:TILE] = exposed(fine[80 * z : 80 * z + CYC])
        a_ref[z, :, TILE:WIDE] = side[0:CYC, 128 * z : 128 * (z + 1)]
        q_ref[z, STRIP:CYC, 0:TILE] = ring_ref[z]
        q_ref[z, :, TILE:WIDE] = side_q[0:CYC, 128 * z : 128 * (z + 1)]
    copy.wait()
    for z in range(PLANES):
        a_mid[z], q_mid[z] = moved(a_ref, q_ref, z, CYC, WIDE)
    copies = []
    for z in range(PLANES):
        a_end[z], q_end[z] = moved(a_mid, q_mid, z, STRIP, TILE)
        for i, (src, dst) in enumerate(((a_end, a_out), (q_end, q_out))):
            copies.append(pltpu.make_async_copy(src.at[z], dst.at[z], sem.at[1 + i, z]))
            copies[-1].start()
    for copy in copies:
        copy.wait()


def patch_kernel(tile_ref, m_ref, a_in, q_in, a_out, q_out, a_ref, q_ref, a_mid, q_mid, a_end, q_end, sem):
    level = lax.axis_index("depth")
    last = level == 7

    def redo(start, outer, away):
        spot = pl.ds(start, 8)
        copies = [
            pltpu.make_async_copy(a_out.at[:, spot, :], a_end, sem.at[0]),
            pltpu.make_async_copy(q_out.at[:, spot, :], q_end, sem.at[1]),
        ]
        for copy in copies:
            copy.start()
        m = m_ref[...].astype(F32)
        for z in range(PLANES):
            for f, ref in ((0, a_ref), (1, q_ref)):
                ref[z, 0:8, :] = tile_ref[f, z]
                ref[z, 8:16, :] = jnp.zeros((8, WIDE), F32)
                ref[z, away : away + 2, :] = m[16 * f + 2 * z : 16 * f + 2 * z + 2]
        for z in range(PLANES):
            a_mid[z], q_mid[z] = moved(a_ref, q_ref, z, 16, WIDE)
        for copy in copies:
            copy.wait()
        for z in range(PLANES):
            a, q = moved(a_mid, q_mid, z, 8, TILE)
            a_end[z, outer : outer + 2, :] = a[outer : outer + 2]
            q_end[z, outer : outer + 2, :] = q[outer : outer + 2]
        copies = [
            pltpu.make_async_copy(a_end, a_out.at[:, spot, :], sem.at[2]),
            pltpu.make_async_copy(q_end, q_out.at[:, spot, :], sem.at[3]),
        ]
        for copy in copies:
            copy.start()
        for copy in copies:
            copy.wait()

    @pl.when(level == 0)
    def _():
        redo(0, 0, 14)

    @pl.when(last)
    def _():
        redo(STRIP - 8, 6, 8)


ANY = pl.BlockSpec(memory_space=pl.ANY)
HBM = pl.BlockSpec(memory_space=pltpu.HBM)


def call(kernel, out, specs, scratch=(), outs=None, flops=0, size=0, limit=LIMIT, **more):
    return pl.pallas_call(
        kernel,
        out_shape=out,
        in_specs=specs,
        out_specs=jax.tree.map(lambda _: VMEM, out) if outs is None else outs,
        scratch_shapes=scratch,
        compiler_params=pltpu.CompilerParams(vmem_limit_bytes=limit),
        cost_estimate=pl.CostEstimate(flops=flops, bytes_accessed=size, transcendentals=0),
        **more,
    )


def on_device(sizes, mask, kernels, weights, band_rows, band_cols, quencher):
    n_depth, n_tx, n_ty = sizes
    con = constants()
    count = kernels.shape[1]
    shape = jax.ShapeDtypeStruct
    dma = pltpu.SemaphoreType.DMA
    bx = band_rows.reshape(1, BAND)
    by = band_cols.reshape(1, BAND)
    quen = quencher[:, 0]
    table = pltpu.VMEM((256, 256), BF)
    band = pltpu.VMEM((1, BAND), jnp.int32)

    packed = call(
        strip_kernel, shape((8, 128, 128), BF), [HBM] * 2, limit=MOST,
        scratch=[
            pltpu.VMEM((4, STRIP, 128), jnp.int32), pltpu.VMEM((PLANES, 8, TILE), F32),
            pltpu.VMEM((PLANES, 8, TILE), F32), pltpu.VMEM((32, TILE), F32), dma((6,)),
        ],
    )(mask[0], quen)
    got = lax.all_to_all(packed, "depth", 0, 0, tiled=True)
    *tables, cols, placed, side, weight = call(
        table_kernel,
        (
            shape((TILE, 128), BF), *[shape((256, 128), BF)] * 4, shape((128, TILE), BF),
            shape((128, 128 * count), BF), shape((PLANES, 16, STRIP), F32), shape((16, HALF), F32),
        ),
        [ANY] + [HBM] * 9,
        scratch=[
            band, band, pltpu.VMEM((TILE, 256), BF), table, table, table, pltpu.VMEM((16, 256), BF),
            pltpu.VMEM((PLANES, STRIP, TILE), F32), pltpu.SMEM((count,), F32), dma((9,)),
        ],
        flops=400_000_000, size=2_000_000,
    )(packed, bx, by, con["cs"], con["pairs_hi"], con["pairs_lo"], con["even_t"], con["edge"], quen, weights)
    rows = tables[0]
    big, left, right, ring = call(
        spectrum_kernel,
        (
            shape((128, 128 * count), BF), shape((32, TILE), BF), shape((32, TILE), BF),
            shape((PLANES, 8, TILE), F32),
        ),
        [VMEM] * 10,
    )(weight, got, kernels[0], *tables, placed, side)
    from_right = lax.ppermute(left, "ty", [(i, (i - 1) % n_ty) for i in range(n_ty)])
    from_left = lax.ppermute(right, "ty", [(i, (i + 1) % n_ty) for i in range(n_ty)])
    image = call(
        image_kernel, shape((TILE, HALF), F32), [VMEM] * 4, flops=2_400_000_000, size=2_000_000,
    )(weight, big, rows, cols)
    strips = call(
        pack_kernel, shape((8, 80, HALF), BF), [VMEM] * 3, scratch=[pltpu.VMEM((16, HALF), F32)],
    )(image, from_left, from_right)
    planes = lax.all_to_all(strips, "depth", 0, 0, tiled=True)
    tile = pltpu.VMEM((PLANES, 8, TILE), F32)
    edge, outer = call(
        edge_kernel, (shape((2, PLANES, 8, WIDE), F32), shape((32, WIDE), BF)), [VMEM] * 2 + [HBM] + [VMEM] * 2,
        scratch=[tile, tile, pltpu.VMEM((32, WIDE), F32), dma((2,))],
    )(planes, con["spread"], quen, from_left, from_right)
    pairs = []
    for t in range(n_tx):
        low, high = (n_depth - 1) * n_tx + t, (t + 1) % n_tx
        pairs += [(low, high), (high, low)]
    outer = lax.ppermute(outer, ("depth", "tx"), pairs)
    out = shape((PLANES, STRIP, TILE), F32)
    wide = pltpu.VMEM((PLANES, CYC, WIDE), F32)
    end = pltpu.VMEM((PLANES, STRIP, TILE), F32)
    acid, left_over = call(
        bake_kernel, (out, out), [VMEM] * 2 + [HBM] + [VMEM] * 3, outs=(HBM, HBM),
        scratch=[wide, wide, wide, wide, end, end, dma((3, PLANES))], flops=3_000_000_000, size=4_000_000,
    )(planes, con["spread"], quen, ring, from_left, from_right)
    low = pltpu.VMEM((PLANES, 16, WIDE), F32)
    acid, left_over = call(
        patch_kernel, (out, out), [VMEM] * 2 + [HBM] * 2, outs=(HBM, HBM),
        scratch=[low, low, low, low, tile, tile, dma((4,))], input_output_aliases={2: 0, 3: 1},
    )(edge, outer, acid, left_over)
    return acid[:, None], left_over[:, None]


def solution(mesh):
    sizes = (mesh.shape["depth"], mesh.shape["tx"], mesh.shape["ty"])
    placed = (
        P("tx", "depth", "ty"),
        P("depth", None, None, None),
        P(),
        P(),
        P(),
        P(None, "tx", "depth", "ty"),
    )
    return jax.shard_map(
        functools.partial(on_device, sizes),
        mesh=mesh,
        in_specs=placed,
        out_specs=(P(None, "tx", "depth", "ty"), P(None, "tx", "depth", "ty")),
        check_vma=False,
    )
```

time: 248 us -> 64.5 us (0.26)
  the two profiles are of different devices: /device:TPU:17 before, /device:TPU:46 now
where the time goes in v1:
time: 64.5 us; the launch traced here: 64.1 us
  starting transfers between devices  18.2 us (28%)
  Pallas kernels  16.9 us (26%)
  blocking collectives  13.7 us (21%)
  waiting for transfers between devices  13.1 us (20%)
  local copies, waits for them, and re-layouts  1.35 us (2%)
  between operations  0.82 us (1%)
    all_to_all x1, blocking collectives, on_device(): planes = lax.all_to_all(strips, 'depth', 0, 0, tiled=True)  13.7 us
    all_to_all x1, starting transfers between devices, on_device(): got = lax.all_to_all(packed, 'depth', 0, 0, tiled=True)  10.5 us
    all_to_all x1, waiting for transfers between devices, on_device(): got = lax.all_to_all(packed, 'depth', 0, 0, tiled=True)  8.5 us
    pallas_call x1, Pallas kernels, on_device(): call(bake_kernel, (out, out), [VMEM] * 2 + [HBM] + [VMEM] * 3, outs=(HBM,...  5.86 us
    ppermute x1, starting transfers between devices, on_device(): lax.ppermute(right, 'ty', [(i, (i + 1) % n_ty) for i in range(n_ty)])  3.16 us
    ppermute x1, waiting for transfers between devices, on_device(): lax.ppermute(left, 'ty', [(i, (i - 1) % n_ty) for i in range(n_ty)])  2.89 us
    ppermute x1, starting transfers between devices, on_device(): lax.ppermute(left, 'ty', [(i, (i - 1) % n_ty) for i in range(n_ty)])  2.67 us
    pallas_call x1, Pallas kernels, on_device(): call(image_kernel, shape((TILE, HALF), F32), [VMEM] * 4, flops=2400000000...  2.33 us
  transfers between devices with their start and end apart: 4, of which 3 were waited for; matrix products, arithmetic and copies ran while one was open for 0% of the time, Pallas kernels for 16%

profile of v1, /device:TPU:46, one launch (start us, length us, event | category | flops | bytes accessed | tf_op | source)
XLA Modules:
  0.0 64.1 jit_solution(6993585952837557876)
XLA Ops:
  0.6 0.0 copy-start.5
  0.7 0.0 copy-start.6
  0.7 0.0 copy-start.7
  0.7 1.9 %shard_map.131.after = bf16[8,128,128]{2,1,0:T(8,128)(2,1)} custom-call(s32[64,512]{1,0:T(8,128)} %bitcast.20, f32[8,64,512]{2,1,0:T(8,128)} %bitcast.11), custom_call_target="tpu_custom_call" | custom-call | tf_op jit(solution)/shard_map/pallas_call | solution.py:415
  2.6 0.0 copy-start.3
  2.6 10.5 %all-to-all-start = ((bf16[8,128,128]{2,1,0:T(8,128)(2,1)}), bf16[8,128,128]{2,1,0:T(8,128)(2,1)S(1)}, u32[]{:S(2)}, u32[]{:S(2)}) async-start(bf16[8,128,128]{2,1,0:T(8,128)(2,1)} %shard_map.131.after), calls=%async_computation | async-start | bytes 524288 | tf_op jit(solution)/shard_map/all_to_all | solution.py:422
  13.2 0.6 copy-done.9
  13.8 0.0 copy-done.10
  13.8 0.0 copy-done.11
  13.8 0.7 %copy-done.8 = bf16[16,256]{1,0:T(8,128)(2,1)S(1)} copy-done((bf16[16,256]{1,0:T(8,128)(2,1)S(1)}, bf16[16,256]{1,0:T(8,128)(2,1)}, u32[]{:S(2)}) %copy-start.8) | copy-done | bytes 8216
  14.5 2.0 %shard_map.132 = (bf16[512,128]{1,0:T(8,128)(2,1)S(1)}, bf16[256,128]{1,0:T(8,128)(2,1)S(1)}, bf16[256,128]{1,0:T(8,128)(2,1)S(1)}, bf16[256,128]{1,0:T(8,128)(2...) custom-call(bf16[8,128,128]{2,1,0:T(8,128)(2,1)S(1)} %copy-done.1, ...), custom_call_target="tpu_custom_call" | custom-call | flops 400000000 | bytes 2000000 | tf_op jit(solution)/shard_map/pallas_call | solution.py:423
  16.5 8.5 %all-to-all-done.got_ref = bf16[8,128,128]{2,1,0:T(8,128)(2,1)S(1)} async-done(((bf16[8,128,128]{2,1,0:T(8,128)(2,1)}), bf16[8,128,128]{2,1,0:T(8,128)(2,1)S(1)}, u32[]{:S(2)}, u32[]{:S(2)}) %all-to-all-start) | async-done | bytes 262176 | tf_op jit(solution)/shard_map/all_to_all | solution.py:422
  25.0 1.5 %shard_map.133 = (bf16[128,1536]{1,0:T(8,128)(2,1)S(1)}, bf16[32,512]{1,0:T(8,128)(2,1)S(1)}, bf16[32,512]{1,0:T(8,128)(2,1)S(1)}, f32[8,8,512]{2,1,0:T(8,128)S(1)}) custom-call(f32[16,256]{1,0:T(8,128)S(1)} %get-tuple-element.21.w_ref, bf16[8,128,128]{2,1,0:T(8,128)(2,1)S(1)} %all-to-all-done.got_ref, bf16[12,64,128]{2,1,0:T(8,128)(2,1)S(1)} %bitcast.15, ...), custom_call_target="tpu_custom_call" | custom-call | tf_op jit(solution)/shard_map/pallas_call | solution.py:437
  26.5 3.2 %collective-permute-start = (bf16[32,512]{1,0:T(8,128)(2,1)S(1)}, bf16[32,512]{1,0:T(8,128)(2,1)S(1)}, u32[]{:S(2)}, u32[]{:S(2)}) collective-permute-start(bf16[32,512]{1,0:T(8,128)(2,1)S(1)} %get-tuple-element.31), channel_id=1, source_target_pairs={{0,1},{1,2},{2,3},{3,4},{4,5},{5,6},{6,7},{7,0},{8,9},{9,10},{10,1... | collective-permute-start | bytes 98312 | tf_op jit(solution)/shard_map/ppermute | solution.py:446
  29.7 2.7 %collective-permute-start.1 = (bf16[32,512]{1,0:T(8,128)(2,1)S(1)}, bf16[32,512]{1,0:T(8,128)(2,1)S(1)}, u32[]{:S(2)}, u32[]{:S(2)}) collective-permute-start(bf16[32,512]{1,0:T(8,128)(2,1)S(1)} %get-tuple-element.32), channel_id=1, source_target_pairs={{0,7},{1,0},{2,1},{3,2},{4,3},{5,4},{6,5},{7,6},{8,15},{9,8},{10,9... | collective-permute-start | bytes 98312 | tf_op jit(solution)/shard_map/ppermute | solution.py:445
  32.4 2.3 %shard_map.134.img_ref = f32[512,256]{1,0:T(8,128)S(1)} custom-call(f32[16,256]{1,0:T(8,128)S(1)} %get-tuple-element.21.w_ref, bf16[128,1536]{1,0:T(8,128)(2,1)S(1)} %get-tuple-element.29.big_ref, bf16[512,128]{1,0:T(8,128)(2,1)S(1)} %get-tuple-element.22.rows_ref, bf16[128,512]{1,0:T(8,128)(2,1)S(1)} %get-tuple-element.30.cols_ref), custom_call_target="tpu_custom_call" | custom-call | flops 2400000000 | bytes 2000000 | tf_op jit(solution)/shard_map/pallas_call | solution.py:447
  34.7 2.9 %collective-permute-done.1.from_right = bf16[32,512]{1,0:T(8,128)(2,1)S(1)} collective-permute-done((bf16[32,512]{1,0:T(8,128)(2,1)S(1)}, bf16[32,512]{1,0:T(8,128)(2,1)S(1)}, u32[]{:S(2)}, u32[]{:S(2)}) %collective-permute-start.1) | collective-permute-done | bytes 32800 | tf_op jit(solution)/shard_map/ppermute | solution.py:445
  37.6 0.1 shard_map.135
  37.8 13.7 %all_to_all.10.got_ref = bf16[8,80,256]{2,1,0:T(8,128)(2,1)S(1)} all-to-all(bf16[8,80,256]{2,1,0:T(8,128)(2,1)S(1)} %shard_map.135), channel_id=1, replica_groups=mesh['depth'=8,'tx'=8,'ty'=8] {'depth'}, dimensions={0} | all-to-all | bytes 655360 | tf_op jit(solution)/shard_map/all_to_all | solution.py:453
  51.4 1.2 %shard_map.136 = (f32[2,8,8,640]{3,2,1,0:T(8,128)S(1)}, bf16[32,640]{1,0:T(8,128)(2,1)S(1)}) custom-call(bf16[8,80,256]{2,1,0:T(8,128)(2,1)S(1)} %all_to_all.10.got_ref, bf16[512,512]{1,0:T(8,128)(2,1)S(1)} %copy-done.2, f32[8,64,512]{2,1,0:T(8,128)S(1)} %bitcast.13, bf16[32,512]{1,0:T(8,128)(2,1)S(1)} %collective-permute-done.from_left, ...), custom_call_target="tpu_custom_call" | custom-call | tf_op jit(solution)/shard_map/pallas_call | solution.py:455
  52.6 1.9 %collective-permute-start.2 = (bf16[32,640]{1,0:T(8,128)(2,1)S(1)}, bf16[32,640]{1,0:T(8,128)(2,1)S(1)}, u32[]{:S(2)}, u32[]{:S(2)}) collective-permute-start(bf16[32,640]{1,0:T(8,128)(2,1)S(1)} %get-tuple-element.34), channel_id=1, source_target_pairs={{448,8},{8,448},{456,16},{16,456},{464,24},{24,464},{472,32},{32,4... | collective-permute-start | bytes 122888 | tf_op jit(solution)/shard_map/ppermute | solution.py:463
  54.5 5.9 %shard_map.137 = (f32[8,64,512]{2,1,0:T(8,128)}, f32[8,64,512]{2,1,0:T(8,128)}) custom-call(bf16[8,80,256]{2,1,0:T(8,128)(2,1)S(1)} %all_to_all.10.got_ref, bf16[512,512]{1,0:T(8,128)(2,1)S(1)} %copy-done.2, f32[8,64,512]{2,1,0:T(8,128)S(1)} %bitcast.14, f32[8,8,512]{2,1,0:T(8,128)S(1)} %get-tuple-element.35.ring_ref, ...), custom_call_target="tpu_custom_call" | custom-call | flops 3000000000 | bytes 4000000 | tf_op jit(solution)/shard_map/pallas_call | solution.py:467
  60.4 1.7 %collective-permute-done.2.m_ref = bf16[32,640]{1,0:T(8,128)(2,1)S(1)} collective-permute-done((bf16[32,640]{1,0:T(8,128)(2,1)S(1)}, bf16[32,640]{1,0:T(8,128)(2,1)S(1)}, u32[]{:S(2)}, u32[]{:S(2)}) %collective-permute-start.2) | collective-permute-done | bytes 40992 | tf_op jit(solution)/shard_map/ppermute | solution.py:463
  62.2 1.9 %shard_map.138 = (f32[8,64,512]{2,1,0:T(8,128)}, f32[8,64,512]{2,1,0:T(8,128)}) custom-call(f32[2,8,8,640]{3,2,1,0:T(8,128)S(1)} %get-tuple-element.33.tile_ref, bf16[32,640]{1,0:T(8,128)(2,1)S(1)} %collective-permute-done.2.m_ref, f32[8,64,512]{2,1,0:T(8,128)} %get-tuple-element.36.a_in, ...), custom_call_target="tpu_custom_call", output_to_operand_aliasing={{0}: (2, {}), {1}: (3, {})} | custom-call | tf_op jit(solution)/shard_map/pallas_call | solution.py:472
  (17 shorter events, 0.0 us)
Async XLA Ops:
  0.6 12.5 %copy-start = (f32[8,1,64,512]{3,2,1,0:T(8,128)S(1)}, f32[8,1,64,512]{3,2,1,0:T(8,128)}, u32[]{:S(2)}) copy-start(f32[8,1,64,512]{3,2,1,0:T(8,128)} %param.17) | copy-start | bytes 3145732
  0.6 12.5 %copy-start.5 = (bf16[256,256]{1,0:T(8,128)(2,1)S(1)}, bf16[256,256]{1,0:T(8,128)(2,1)}, u32[]{:S(2)}) copy-start(bf16[256,256]{1,0:T(8,128)(2,1)} %constant.15.clone.even_in) | copy-start | bytes 393220
  0.7 12.5 %copy-start.6 = (bf16[256,256]{1,0:T(8,128)(2,1)S(1)}, bf16[256,256]{1,0:T(8,128)(2,1)}, u32[]{:S(2)}) copy-start(bf16[256,256]{1,0:T(8,128)(2,1)} %constant.14.clone.lo_in) | copy-start | bytes 393220
  0.7 12.5 %copy-start.7 = (bf16[256,256]{1,0:T(8,128)(2,1)S(1)}, bf16[256,256]{1,0:T(8,128)(2,1)}, u32[]{:S(2)}) copy-start(bf16[256,256]{1,0:T(8,128)(2,1)} %constant.13.clone.hi_in) | copy-start | bytes 393220
  2.6 10.6 %copy-start.1 = (bf16[8,128,128]{2,1,0:T(8,128)(2,1)S(1)}, bf16[8,128,128]{2,1,0:T(8,128)(2,1)}, u32[]{:S(2)}) copy-start(bf16[8,128,128]{2,1,0:T(8,128)(2,1)} %shard_map.131.after) | copy-start | bytes 786436
  2.6 10.6 %copy-start.3 = (bf16[512,256]{1,0:T(8,128)(2,1)S(1)}, bf16[512,256]{1,0:T(8,128)(2,1)}, u32[]{:S(2)}) copy-start(bf16[512,256]{1,0:T(8,128)(2,1)} %constant.12.clone.cs_in) | copy-start | bytes 786436
  2.6 22.3 %all-to-all-start = ((bf16[8,128,128]{2,1,0:T(8,128)(2,1)}), bf16[8,128,128]{2,1,0:T(8,128)(2,1)S(1)}, u32[]{:S(2)}, u32[]{:S(2)}) async-start(bf16[8,128,128]{2,1,0:T(8,128)(2,1)} %shard_map.131.after), calls=%async_computation | async-start | bytes 524288 | tf_op jit(solution)/shard_map/all_to_all | solution.py:422
  13.1 0.7 %copy-start.9 = (s32[64]{0:T(128)S(1)}, s32[64]{0:T(128)}, u32[]{:S(2)}) copy-start(s32[64]{0:T(128)} %param.15) | copy-start | bytes 772
  13.1 0.7 %copy-start.10 = (s32[64]{0:T(128)S(1)}, s32[64]{0:T(128)}, u32[]{:S(2)}) copy-start(s32[64]{0:T(128)} %param.16) | copy-start | bytes 772
  13.1 0.7 %copy-start.11 = (f32[12]{0:T(128)S(1)}, f32[12]{0:T(128)}, u32[]{:S(2)}) copy-start(f32[12]{0:T(128)} %w_in.1) | copy-start | bytes 148
  13.8 0.7 %copy-start.8 = (bf16[16,256]{1,0:T(8,128)(2,1)S(1)}, bf16[16,256]{1,0:T(8,128)(2,1)}, u32[]{:S(2)}) copy-start(bf16[16,256]{1,0:T(8,128)(2,1)} %constant.16.clone.edge_in) | copy-start | bytes 24580
  14.5 10.5 %copy-start.4 = (bf16[1,12,64,128]{3,2,1,0:T(8,128)(2,1)S(1)}, bf16[1,12,64,128]{3,2,1,0:T(8,128)(2,1)}, u32[]{:S(2)}) copy-start(bf16[1,12,64,128]{3,2,1,0:T(8,128)(2,1)} %param.13) | copy-start | bytes 589828
  26.5 8.2 %collective-permute-start = (bf16[32,512]{1,0:T(8,128)(2,1)S(1)}, bf16[32,512]{1,0:T(8,128)(2,1)S(1)}, u32[]{:S(2)}, u32[]{:S(2)}) collective-permute-start(bf16[32,512]{1,0:T(8,128)(2,1)S(1)} %get-tuple-element.31), channel_id=1, source_target_pairs={{0,1},{1,2},{2,3},{3,4},{4,5},{5,6},{6,7},{7,0},{8,9},{9,10},{10,1... | collective-permute-start | bytes 98312 | tf_op jit(solution)/shard_map/ppermute | solution.py:446
  29.7 7.9 %collective-permute-start.1 = (bf16[32,512]{1,0:T(8,128)(2,1)S(1)}, bf16[32,512]{1,0:T(8,128)(2,1)S(1)}, u32[]{:S(2)}, u32[]{:S(2)}) collective-permute-start(bf16[32,512]{1,0:T(8,128)(2,1)S(1)} %get-tuple-element.32), channel_id=1, source_target_pairs={{0,7},{1,0},{2,1},{3,2},{4,3},{5,4},{6,5},{7,6},{8,15},{9,8},{10,9... | collective-permute-start | bytes 98312 | tf_op jit(solution)/shard_map/ppermute | solution.py:445
  37.7 13.7 %copy-start.2 = (bf16[512,512]{1,0:T(8,128)(2,1)S(1)}, bf16[512,512]{1,0:T(8,128)(2,1)}, u32[]{:S(2)}) copy-start(bf16[512,512]{1,0:T(8,128)(2,1)} %constant.17.clone.spread_ref) | copy-start | bytes 1572868
  52.6 9.5 %collective-permute-start.2 = (bf16[32,640]{1,0:T(8,128)(2,1)S(1)}, bf16[32,640]{1,0:T(8,128)(2,1)S(1)}, u32[]{:S(2)}, u32[]{:S(2)}) collective-permute-start(bf16[32,640]{1,0:T(8,128)(2,1)S(1)} %get-tuple-element.34), channel_id=1, source_target_pairs={{448,8},{8,448},{456,16},{16,456},{464,24},{24,464},{472,32},{32,4... | collective-permute-start | bytes 122888 | tf_op jit(solution)/shard_map/ppermute | solution.py:463

commit v2 on v1

v2 whole, which is shorter than its diff:
```python
import functools
import math

import jax
import jax.numpy as jnp
import numpy as np
from jax import lax
from jax.experimental import pallas as pl
from jax.experimental.pallas import tpu as pltpu
from jax.sharding import PartitionSpec as P

BF = jnp.bfloat16
F32 = jnp.float32
TILE = 512
BAND = 64
HALF = 256
PLANES = 8
STRIP = 64
CYC = 72
WIDE = 640
DILL_RATE = 1.0
REACT_RATE = 0.4
ACID_LAT, ACID_VERT = 0.23, 0.03
QUEN_LAT, QUEN_VERT = 0.15, 0.05
VMEM = pl.BlockSpec(memory_space=pltpu.VMEM)
SMEM = pl.BlockSpec(memory_space=pltpu.SMEM)
LIMIT = 40 * 1024 * 1024
MOST = 60 * 1024 * 1024


def split(x):
    hi = np.asarray(x, np.float32).astype(jnp.bfloat16)
    lo = (np.asarray(x, np.float64) - hi.astype(np.float64)).astype(np.float32).astype(jnp.bfloat16)
    return hi, lo


@functools.cache
def constants():
    u = np.arange(TILE)
    f = np.arange(128) - BAND // 2
    angle = np.mod(u[:, None] * f[None, :], TILE) * (2.0 * np.pi / TILE)
    cs = np.concatenate([np.cos(angle), np.sin(angle)], 1)
    n = np.arange(HALF)
    m = np.arange(1, 128)
    gap = np.mod(u[None, :] - 2 * n[:, None], TILE)
    line = (1.0 + 2.0 * np.cos(2.0 * np.pi * m[None, :] * u[:, None] / TILE).sum(1)) / HALF
    spread = line[gap]
    spread[:, 0::2] = np.eye(HALF)
    out = {}
    out["cs"] = split(cs)[0]
    out["pairs_hi"], out["pairs_lo"] = split(cs[0::2] + cs[1::2])
    out["even_t"] = split(cs[0::2].T)[0]
    edge = np.zeros((16, 256))
    edge[:4] = cs[[0, 1, TILE - 2, TILE - 1]]
    out["edge"] = split(edge)[0]
    out["spread"] = np.concatenate(split(spread), 0)
    return out


def dot(a, b):
    return lax.dot_general(a, b, (((1,), (0,)), ((), ())), preferred_element_type=F32)


def dot_nt(a, b):
    return lax.dot_general(a, b, (((1,), (1,)), ((), ())), preferred_element_type=F32)


def dot_tn(a, b):
    return lax.dot_general(a, b, (((0,), (0,)), ((), ())), preferred_element_type=F32)


def iota(shape, dim):
    return lax.broadcasted_iota(jnp.int32, shape, dim)


def fetch(sem, *pairs):
    copies = [pltpu.make_async_copy(src, dst, sem.at[i]) for i, (src, dst) in enumerate(pairs)]
    for copy in copies:
        copy.start()
    return copies


def picker(band_ref):
    band = band_ref[...]
    return (iota((256, 128), 0) == jnp.concatenate([band, band + 128], 1)).astype(BF)


def columns():
    row = iota((16, TILE), 0)
    col = jnp.where(row < 2, row, row + TILE - 4)
    return ((iota((16, TILE), 1) == col) & (row < 4)).astype(BF)


def strip_kernel(mask_in, quen_in, out_ref, mask, head, tail, edge, sem):
    copies = fetch(
        sem, *[(mask_in.at[:, pl.ds(128 * c, 128)], mask.at[c]) for c in range(4)],
        (quen_in.at[:, pl.ds(0, 8), :], head), (quen_in.at[:, pl.ds(STRIP - 8, 8), :], tail),
    )
    halves = (iota((TILE, HALF), 0) == 2 * iota((TILE, HALF), 1)).astype(BF)
    for copy in copies[:4]:
        copy.wait()
    rows = [mask[c, pl.ds(0, STRIP // 2, stride=2), :] for c in range(4)]
    coarse = dot(jnp.concatenate(rows, 1).astype(F32).astype(BF), halves).astype(BF)
    for copy in copies[4:]:
        copy.wait()
    for peer in range(8):
        out_ref[peer, 0:32, :] = coarse[:, 0:128]
        out_ref[peer, 32:64, :] = coarse[:, 128:256]
        for k, c in enumerate((0, 2, 1, 3)):
            edge[peer, 4 * k : 4 * k + 2, :] = head[peer, 0:2, 128 * c : 128 * (c + 1)]
            edge[peer, 4 * k + 2 : 4 * k + 4, :] = tail[peer, 6:8, 128 * c : 128 * (c + 1)]
        out_ref[peer, 64:80, :] = edge[peer].astype(BF)


def table_kernel(
    after, bx_in, by_in, cs_in, hi_in, lo_in, even_in, edge_in, quen_in, w_in,
    rows_ref, xhi_ref, xlo_ref, yhi_ref, ylo_ref, cols_ref, placed_ref, left_ref, right_ref, weight_ref,
    bx, by, cs, hi_tab, lo_tab, even, edge, quen, w, sem,
):
    copies = fetch(
        sem, (bx_in, bx), (by_in, by), (edge_in, edge), (even_in, even), (cs_in, cs), (hi_in, hi_tab), (lo_in, lo_tab),
        (w_in, w), (quen_in, quen),
    )
    for copy in copies[:8]:
        copy.wait()
    pick_x = picker(bx)
    pick_y = picker(by)
    rows_ref[...] = dot(cs[...], pick_x).astype(BF)
    xhi_ref[...] = dot(hi_tab[...], pick_x).astype(BF)
    xlo_ref[...] = dot(lo_tab[...], pick_x).astype(BF)
    yhi_ref[...] = dot(hi_tab[...], pick_y).astype(BF)
    ylo_ref[...] = dot(lo_tab[...], pick_y).astype(BF)
    table = dot_tn(pick_y, even[...])
    flip = jnp.where(iota((128, 1), 0) < BAND, 1.0, -1.0).astype(F32)
    cols_ref[:, 0:HALF] = (table * flip).astype(BF)
    cols_ref[:, HALF:TILE] = jnp.concatenate([table[BAND:], table[:BAND]], 0).astype(BF)
    sign = jnp.where(iota((1, 128), 1) < BAND, 1.0, -1.0).astype(F32)
    ends = dot(edge[...], pick_y)[0:8]
    ends = jnp.where(iota((8, 128), 0) < 4, sign * ends, pltpu.roll(pltpu.roll(ends, BAND, 1), 4, 0))
    count = placed_ref.shape[1] // 128
    own = iota((128, 128), 0) >> 3
    many = jnp.tile(ends, (16, 1))
    for k in range(count):
        placed_ref[:, 128 * k : 128 * (k + 1)] = jnp.where(own == k, many, 0.0).astype(BF)
        weight_ref[k : k + 1, :] = jnp.full((1, HALF), w[k], F32)
    copies[8].wait()
    ends = dot_nt(columns(), quen[...].reshape(PLANES * STRIP, TILE).astype(BF))
    for low, ref in ((0, left_ref), (2, right_ref)):
        ref[...] = jnp.zeros((16, 128), F32)
        for z in range(PLANES):
            ref[2 * z : 2 * z + 2, 0:STRIP] = ends[low : low + 2, STRIP * z : STRIP * (z + 1)]


def spectrum_kernel(
    w_ref, got_ref, kern_ref, rows_ref, xhi_ref, xlo_ref, yhi_ref, ylo_ref, placed_ref, qleft_ref, qright_ref,
    big_ref, left_ref, right_ref, ring_ref,
):
    lane = iota((1, 128), 1)
    sign = jnp.where(lane < BAND, -1.0, 1.0).astype(F32)
    coarse = jnp.concatenate([got_ref[:, 0:32, :].reshape(256, 128), got_ref[:, 32:64, :].reshape(256, 128)], 1)
    summed = dot(coarse, yhi_ref[...]) + dot(coarse, ylo_ref[...])
    hi = summed.astype(BF)
    lo = (summed - hi.astype(F32)).astype(BF)
    u = (dot_tn(xhi_ref[...], hi) + dot_tn(xhi_ref[...], lo) + dot_tn(xlo_ref[...], hi)) * (1.0 / (TILE * TILE))
    v = u[:BAND] + sign * pltpu.roll(u[BAND:], BAND, 1)
    v_swap = pltpu.roll(v, BAND, 1)
    coef_a = jnp.where(lane < BAND, v, v_swap)
    coef_b = jnp.where(lane < BAND, v_swap, -v)
    count = kern_ref.shape[0]
    for k in range(count):
        cur = kern_ref[k].astype(F32)
        top = cur * coef_a + pltpu.roll(cur, BAND, 1) * coef_b
        big_ref[0:BAND, 128 * k : 128 * (k + 1)] = top.astype(BF)
        big_ref[BAND:128, 128 * k : 128 * (k + 1)] = (sign * pltpu.roll(top, BAND, 1)).astype(BF)
    narrow = dot_nt(placed_ref[...], big_ref[...]).astype(BF)
    field = dot_nt(narrow, rows_ref[...])
    total = jnp.zeros((8, TILE), F32)
    for k in range(count):
        part = field[8 * k : 8 * (k + 1)]
        total = total + w_ref[k : k + 1, 0:1] * (part * part)
    bright = total + pltpu.roll(total, 4, 0)
    place = iota((16, TILE), 0)
    eight = jnp.concatenate([bright, bright], 0)
    left_ref[0:16, :] = jnp.where(place < 2, eight, 0.0).astype(BF)
    right_ref[0:16, :] = jnp.where(place < 2, pltpu.roll(eight, 14, 0), 0.0).astype(BF)
    for ref, cols in ((left_ref, qleft_ref), (right_ref, qright_ref)):
        ref[16:32, 0:128] = cols[...].astype(BF)
        ref[16:32, 128:TILE] = jnp.zeros((16, TILE - 128), BF)
    beyond = (iota((16, 128), 0) & 3) < 2
    heard = [got_ref[p, 64:80, :].astype(F32) for p in range(8)]
    for p in range(0, 8, 2):
        pair = [jnp.where(beyond, heard[(d + 1) % 8], heard[(d + 7) % 8]) for d in (p, p + 1)]
        for d, ring in zip((p, p + 1), pair):
            ring_ref[d, :, 0:128] = ring[0:8]
            ring_ref[d, :, 128:256] = ring[8:16]
        left_ref[32:48, 64 * p : 64 * p + 128] = jnp.concatenate([pair[0][0:8], pair[1][0:8]], 0).astype(BF)
        right_ref[32:48, 64 * p : 64 * p + 128] = jnp.concatenate([pair[0][8:16], pair[1][8:16]], 0).astype(BF)


def image_kernel(w_ref, big_ref, rows_ref, cols_ref, img_ref):
    count = big_ref.shape[1] // 128
    chunk = 128
    cols = cols_ref[...]
    for part in range(TILE // chunk):
        half = dot(rows_ref[part * chunk : (part + 1) * chunk, :], big_ref[...]).astype(BF)
        total = jnp.zeros((chunk, HALF), F32)
        for k in range(count):
            field = dot(half[:, 128 * k : 128 * (k + 1)], cols)
            total = total + w_ref[k : k + 1, :] * (field[:, :HALF] * field[:, :HALF] + field[:, HALF:] * field[:, HALF:])
        img_ref[part * chunk : (part + 1) * chunk, :] = total


def pack_kernel(img_ref, ring_ref, from_left, from_right, out_ref, scr_ref):
    place = iota((8, TILE), 0)
    both = jnp.where(place < 2, from_left[0:16, :].astype(F32)[0:8], pltpu.roll(from_right[0:16, :].astype(F32)[0:8], 2, 0))
    far = from_left[32:48, :].astype(F32)
    near = from_right[32:48, :].astype(F32)
    lane = iota((8, 128), 1)
    for p in range(8):
        base = p * STRIP
        out_ref[p, 0:STRIP, :] = img_ref[base : base + STRIP, :].astype(BF)
        nxt = (base + STRIP) % TILE
        scr_ref[0:2, :] = img_ref[nxt : nxt + 2, :]
        prv = (base - 2) % TILE
        scr_ref[6:8, :] = img_ref[prv : prv + 2, :]
        first = pltpu.roll(both, (TILE - base) % TILE, 1)[:, 0:128]
        second = pltpu.roll(both, (TILE - base + CYC) % TILE, 1)[:, 0:128]
        side = jnp.where(lane < 66, first, jnp.where(lane < CYC, second, 0.0))
        scr_ref[2:6, 0:128] = side[0:4]
        spot, cols = 8 * (p & 1), slice(128 * (p >> 1), 128 * (p >> 1) + 128)
        corner = jnp.where(lane < STRIP, near[spot : spot + 8, cols], pltpu.roll(far[spot : spot + 8, cols], 4, 0))
        scr_ref[2:6, 128:HALF] = corner[0:4]
        scr_ref[8:16, :] = ring_ref[p]
        out_ref[p, STRIP:80, :] = scr_ref[...].astype(BF)


def acid_side(got_ref):
    return got_ref[:, 64:80, 0:128].astype(F32).reshape(16 * PLANES, 128).T


def acid_cols(side, z):
    return pltpu.roll(side, (124 - 16 * z) % 128, 1)


def quen_side(from_left, from_right):
    both = [from_left[16:32, 0:128].astype(F32), from_right[16:32, 0:128].astype(F32), jnp.zeros((96, 128), F32)]
    return jnp.concatenate(both, 0).T


def quen_cols(side, z):
    behind = iota((1, 128), 1) >= STRIP
    return jnp.where(behind, pltpu.roll(side, (126 - 2 * z) % 128, 1), pltpu.roll(side, (112 - 2 * z) % 128, 1))


def exposed(intensity):
    return 1.0 - jnp.exp(-DILL_RATE * intensity)


def edge_kernel(after, got_ref, spread_ref, quen_in, from_left, from_right, tile_ref, m_ref, near, far, scr, sem):
    copies = fetch(sem, (quen_in.at[:, pl.ds(0, 8), :], near), (quen_in.at[:, pl.ds(STRIP - 8, 8), :], far))
    last = lax.axis_index("depth") == 7
    start = pl.multiple_of(jnp.where(last, STRIP - 16, 0), 16)
    coarse = [got_ref[z, pl.ds(start, 16), :] for z in range(PLANES)] + [got_ref[z, 64:80, :] for z in range(PLANES)]
    coarse = jnp.concatenate(coarse, 0)
    fine = exposed(dot(jnp.concatenate([coarse, coarse], 1), spread_ref[...]))
    side = acid_side(got_ref)
    side = exposed(jnp.concatenate([jnp.where(last, side[STRIP - 8 : STRIP], side[0:8]), side[STRIP:CYC]], 0))
    side_q = quen_side(from_left, from_right)
    side_q = jnp.where(last, side_q[STRIP - 8 : STRIP], side_q[0:8])
    for z in range(PLANES):
        outer = acid_cols(side, z)
        mine = fine[16 * z : 16 * (z + 1)]
        tile_ref[0, z, :, 0:TILE] = jnp.where(last, mine[8:16], mine[0:8])
        tile_ref[0, z, :, TILE:WIDE] = outer[0:8]
        tile_ref[1, z, :, TILE:WIDE] = quen_cols(side_q, z)
        ring = got_ref[z, 64:80, :].astype(F32)
        back = fine[128 + 16 * z : 136 + 16 * z]
        place = slice(2 * z, 2 * z + 2)
        scr[place, 0:TILE] = jnp.where(last, back[0:2], back[6:8])
        scr[place, TILE:WIDE] = jnp.where(last, outer[8:10], outer[14:16])
        place = slice(16 + 2 * z, 18 + 2 * z)
        scr[place, 0:HALF] = jnp.where(last, ring[8:10], ring[10:12])
        scr[place, HALF:TILE] = jnp.where(last, ring[12:14], ring[14:16])
        scr[place, TILE:WIDE] = jnp.where(last, ring[2:4, 128:HALF], ring[4:6, 128:HALF])
    m_ref[...] = scr[...].astype(BF)
    for copy in copies:
        copy.wait()
    for z in range(PLANES):
        tile_ref[1, z, :, 0:TILE] = jnp.where(last, far[z], near[z])


def moved(src_a, src_q, z, t, cols):
    tiles, width = src_a.shape[1] // 8, src_a.shape[2]
    here, before, after = (pl.ds(8 * (i % tiles), 8) for i in (t, t - 1, t + 1))
    row = iota((8, 1), 0)
    a = src_a[z, here, 0:cols]
    q = src_q[z, here, 0:cols]
    react = REACT_RATE * a * q

    def move(c, ref, lat, vert):
        up = ref[min(z + 1, PLANES - 1), here, 0:cols]
        down = ref[max(z - 1, 0), here, 0:cols]
        wide = ref[z, here, :]
        near = pltpu.roll(jnp.where(row == 7, ref[z, before, 0:cols], c), 1, 0)
        near = near + pltpu.roll(jnp.where(row == 0, ref[z, after, 0:cols], c), 7, 0)
        near = near + (pltpu.roll(wide, 1, 1)[:, 0:cols] + pltpu.roll(wide, width - 1, 1)[:, 0:cols])
        return (1.0 - 4.0 * lat - 2.0 * vert) * c + lat * near + vert * (up + down) - react

    return move(a, src_a, ACID_LAT, ACID_VERT), move(q, src_q, QUEN_LAT, QUEN_VERT)


def bake_kernel(
    turn, got_ref, spread_ref, quen_ref, from_left, from_right, *refs,
):
    a_out, q_out, rim_ref, a_ref, q_ref, a_mid, q_mid, a_end, q_end, sem = refs[-10:]

    @pl.when((lax.axis_index("tx") & 1) == turn)
    def _():
        side = exposed(acid_side(got_ref)[0:CYC])
        side_q = quen_side(from_left, from_right)[0:STRIP]
        coarse = got_ref[...].reshape(PLANES * 80, HALF)
        fine = dot(jnp.concatenate([coarse, coarse], 1), spread_ref[...])
        for z in range(PLANES):
            a_ref[z, :, 0:TILE] = exposed(fine[80 * z : 80 * z + CYC])
            a_ref[z, :, TILE:WIDE] = acid_cols(side, z)
            q_ref[z, 0:STRIP, 0:TILE] = quen_ref[z]
            q_ref[z, 0:STRIP, TILE:WIDE] = quen_cols(side_q, z)
            ring = got_ref[z, STRIP:80, :].astype(F32)
            q_ref[z, STRIP:CYC, :] = jnp.zeros((8, WIDE), F32)
            for i, row in ((0, STRIP), (2, 70)):
                q_ref[z, row : row + 2, 0:HALF] = ring[8 + i : 10 + i]
                q_ref[z, row : row + 2, HALF:TILE] = ring[12 + i : 14 + i]
                q_ref[z, row : row + 2, TILE:WIDE] = ring[2 + i : 4 + i, 128:HALF]
        for z in range(PLANES):
            for t in range(CYC // 8):
                spot = pl.ds(8 * t, 8)
                a_mid[z, spot, :], q_mid[z, spot, :] = moved(a_ref, q_ref, z, t, WIDE)
        copies = []
        for z in range(PLANES):
            for t in range(STRIP // 8):
                spot = pl.ds(8 * t, 8)
                a_end[z, spot, :], q_end[z, spot, :] = moved(a_mid, q_mid, z, t, TILE)
            for i, (src, dst) in enumerate(((a_end, a_out), (q_end, q_out))):
                copies.append(pltpu.make_async_copy(src.at[z], dst.at[z], sem.at[i, z]))
                copies[-1].start()
        level = lax.axis_index("depth")
        for edge, start in ((0, 0), (7, STRIP - 8)):

            @pl.when(level == edge)
            def _():
                rim_ref[0] = a_end[:, start : start + 8, :]
                rim_ref[1] = q_end[:, start : start + 8, :]

        for copy in copies:
            copy.wait()


def patch_kernel(tile_ref, m_ref, rim_even, rim_odd, a_in, q_in, a_out, q_out, a_ref, q_ref, a_mid, q_mid, a_end, q_end, sem):
    level = lax.axis_index("depth")
    last = level == 7

    @pl.when((level == 0) | last)
    def _():
        spot = pl.ds(pl.multiple_of(jnp.where(last, STRIP - 8, 0), 8), 8)
        row = iota((8, 1), 0)
        heard = jnp.where(last, row - 2, 5 - row) < 0
        mine = jnp.where(last, row - 6, 1 - row) >= 0
        m = m_ref[...].astype(F32)
        for z in range(PLANES):
            for f, ref in ((0, a_ref), (1, q_ref)):
                pair = m[16 * f + 2 * z : 16 * f + 2 * z + 2]
                ref[z] = jnp.where(heard, jnp.concatenate([pair] * 4, 0), tile_ref[f, z])
        for z in range(PLANES):
            a_mid[z], q_mid[z] = moved(a_ref, q_ref, z, 0, WIDE)
        odd = (lax.axis_index("tx") & 1) == 1
        for z in range(PLANES):
            a, q = moved(a_mid, q_mid, z, 0, TILE)
            a_end[z] = jnp.where(mine, a, jnp.where(odd, rim_odd[0, z], rim_even[0, z]))
            q_end[z] = jnp.where(mine, q, jnp.where(odd, rim_odd[1, z], rim_even[1, z]))
        for copy in fetch(sem, (a_end, a_out.at[:, spot, :]), (q_end, q_out.at[:, spot, :])):
            copy.wait()


ANY = pl.BlockSpec(memory_space=pl.ANY)
HBM = pl.BlockSpec(memory_space=pltpu.HBM)


def call(kernel, out, specs, scratch=(), outs=None, flops=0, size=0, limit=LIMIT, **more):
    return pl.pallas_call(
        kernel,
        out_shape=out,
        in_specs=specs,
        out_specs=jax.tree.map(lambda _: VMEM, out) if outs is None else outs,
        scratch_shapes=scratch,
        compiler_params=pltpu.CompilerParams(vmem_limit_bytes=limit),
        cost_estimate=pl.CostEstimate(flops=flops, bytes_accessed=size, transcendentals=0),
        **more,
    )


def on_device(sizes, mask, kernels, weights, band_rows, band_cols, quencher):
    n_depth, n_tx, n_ty = sizes
    con = constants()
    count = kernels.shape[1]
    shape = jax.ShapeDtypeStruct
    dma = pltpu.SemaphoreType.DMA
    bx = band_rows.reshape(1, BAND)
    by = band_cols.reshape(1, BAND)
    quen = quencher[:, 0]
    table = pltpu.VMEM((256, 256), BF)
    band = pltpu.VMEM((1, BAND), jnp.int32)

    packed = call(
        strip_kernel, shape((8, 80, 128), BF), [HBM] * 2, limit=MOST,
        scratch=[
            pltpu.VMEM((4, STRIP, 128), jnp.int32), pltpu.VMEM((PLANES, 8, TILE), F32),
            pltpu.VMEM((PLANES, 8, TILE), F32), pltpu.VMEM((8, 16, 128), F32), dma((6,)),
        ],
    )(mask[0], quen)
    got = lax.all_to_all(packed, "depth", 0, 0, tiled=True)
    *tables, cols, placed, qleft, qright, weight = call(
        table_kernel,
        (
            shape((TILE, 128), BF), *[shape((256, 128), BF)] * 4, shape((128, TILE), BF),
            shape((128, 128 * count), BF), shape((16, 128), F32), shape((16, 128), F32), shape((16, HALF), F32),
        ),
        [ANY] + [HBM] * 9,
        scratch=[
            band, band, pltpu.VMEM((TILE, 256), BF), table, table, table, pltpu.VMEM((16, 256), BF),
            pltpu.VMEM((PLANES, STRIP, TILE), F32), pltpu.SMEM((count,), F32), dma((9,)),
        ],
        flops=400_000_000, size=2_000_000,
    )(packed, bx, by, con["cs"], con["pairs_hi"], con["pairs_lo"], con["even_t"], con["edge"], quen, weights)
    rows = tables[0]
    big, left, right, ring = call(
        spectrum_kernel,
        (
            shape((128, 128 * count), BF), shape((48, TILE), BF), shape((48, TILE), BF),
            shape((8, 8, HALF), F32),
        ),
        [VMEM] * 11,
    )(weight, got, kernels[0], *tables, placed, qleft, qright)
    from_right = lax.ppermute(left, "ty", [(i, (i - 1) % n_ty) for i in range(n_ty)])
    from_left = lax.ppermute(right, "ty", [(i, (i + 1) % n_ty) for i in range(n_ty)])
    image = call(
        image_kernel, shape((TILE, HALF), F32), [VMEM] * 4, flops=2_400_000_000, size=2_000_000,
    )(weight, big, rows, cols)
    strips = call(
        pack_kernel, shape((8, 80, HALF), BF), [VMEM] * 4, scratch=[pltpu.VMEM((16, HALF), F32)],
    )(image, ring, from_left, from_right)
    planes = lax.all_to_all(strips, "depth", 0, 0, tiled=True)
    tile = pltpu.VMEM((PLANES, 8, TILE), F32)
    out = shape((PLANES, STRIP, TILE), F32)
    wide = pltpu.VMEM((PLANES, CYC, WIDE), F32)
    done = pltpu.VMEM((PLANES, STRIP, TILE), F32)

    def bake(turn, *before):
        return call(
            functools.partial(bake_kernel, turn), (out, out, shape((2, PLANES, 8, TILE), F32)),
            [VMEM] * 5 + [HBM] * len(before), outs=(HBM, HBM, VMEM),
            scratch=[wide, wide, wide, wide, done, done, dma((2, PLANES))], flops=3_000_000_000, size=4_000_000,
            input_output_aliases={5 + i: i for i in range(len(before))},
        )(planes, con["spread"], quen, from_left, from_right, *before)

    acid, left_over, rim_odd = bake(1)
    edge, outer = call(
        edge_kernel, (shape((2, PLANES, 8, WIDE), F32), shape((32, WIDE), BF)), [ANY] + [VMEM] * 2 + [HBM] + [VMEM] * 2,
        scratch=[tile, tile, pltpu.VMEM((32, WIDE), F32), dma((2,))],
    )(rim_odd, planes, con["spread"], quen, from_left, from_right)
    end = (n_depth - 1) * n_tx
    pairs = [(t, (t + 1) % n_tx) for t in range(n_tx)] + [(end + t, end + (t - 1) % n_tx) for t in range(n_tx)]
    outer = lax.ppermute(outer, ("depth", "tx"), pairs)
    acid, left_over, rim_even = bake(0, acid, left_over)
    low = pltpu.VMEM((PLANES, 8, WIDE), F32)
    acid, left_over = call(
        patch_kernel, (out, out), [VMEM] * 4 + [HBM] * 2, outs=(HBM, HBM),
        scratch=[low, low, low, low, tile, tile, dma((2,))], input_output_aliases={4: 0, 5: 1},
    )(edge, outer, rim_even, rim_odd, acid, left_over)
    return acid[:, None], left_over[:, None]


def solution(mesh):
    sizes = (mesh.shape["depth"], mesh.shape["tx"], mesh.shape["ty"])
    placed = (
        P("tx", "depth", "ty"),
        P("depth", None, None, None),
        P(),
        P(),
        P(),
        P(None, "tx", "depth", "ty"),
    )
    return jax.shard_map(
        functools.partial(on_device, sizes),
        mesh=mesh,
        in_specs=placed,
        out_specs=(P(None, "tx", "depth", "ty"), P(None, "tx", "depth", "ty")),
        check_vma=False,
    )
```

time: 64.5 us -> 58.9 us (0.913)
  waiting for transfers between devices: 13.1 us -> 9.35 us
  Pallas kernels: 16.9 us -> 13.8 us
  local copies, waits for them, and re-layouts: 1.35 us -> 2.46 us
    all_to_all x1, waiting for transfers between devices: 8.5 us -> 5.21 us  [on_device(): got = lax.all_to_all(packed, 'depth', 0, 0, tiled=True)]
    pallas_call x5 -> x6, Pallas kernels: 11.4 us -> 9.03 us  [the longest x2 4.57 us: bake(): call(functools.partial(bake_kernel, turn), (out, out, shape((2, PLANES, 8...]
    unnamed x24, local copies, waits for them, and re-layouts: 1.35 us -> 2.46 us
    pallas_call x1, Pallas kernels: 1.17 us -> 0.42 us  [on_device(): call(edge_kernel, (shape((2, PLANES, 8, WIDE), F32), shape((32, WIDE), BF...]
    ppermute x1, waiting for transfers between devices: 1.75 us -> 1.07 us  [on_device(): outer = lax.ppermute(outer, ('depth', 'tx'), pairs)]
  transfers between devices with their start and end apart: 4 -> 4, of which waited for: 3 -> 3; matrix products, arithmetic and copies ran while one was open for 0% -> 0% of each run, Pallas kernels for 16% -> 15%
where the time goes in v2:
time: 58.9 us; the launch traced here: 58.6 us
  starting transfers between devices  18.2 us (31%)
  Pallas kernels  13.8 us (23%)
  blocking collectives  13.7 us (23%)
  waiting for transfers between devices  9.35 us (16%)
  local copies, waits for them, and re-layouts  2.46 us (4%)
  between operations  1 us (2%)
    all_to_all x1, blocking collectives, on_device(): planes = lax.all_to_all(strips, 'depth', 0, 0, tiled=True)  13.7 us
    all_to_all x1, starting transfers between devices, on_device(): got = lax.all_to_all(packed, 'depth', 0, 0, tiled=True)  10.5 us
    all_to_all x1, waiting for transfers between devices, on_device(): got = lax.all_to_all(packed, 'depth', 0, 0, tiled=True)  5.21 us
    pallas_call x2, Pallas kernels, bake(): call(functools.partial(bake_kernel, turn), (out, out, shape((2, PLANES, 8...  4.57 us
    ppermute x1, starting transfers between devices, on_device(): lax.ppermute(right, 'ty', [(i, (i + 1) % n_ty) for i in range(n_ty)])  3.17 us
    ppermute x1, waiting for transfers between devices, on_device(): lax.ppermute(left, 'ty', [(i, (i - 1) % n_ty) for i in range(n_ty)])  3.07 us
    ppermute x1, starting transfers between devices, on_device(): lax.ppermute(left, 'ty', [(i, (i - 1) % n_ty) for i in range(n_ty)])  2.67 us
    unnamed x24, local copies, waits for them, and re-layouts  2.46 us
  transfers between devices with their start and end apart: 4, of which 3 were waited for; matrix products, arithmetic and copies ran while one was open for 0% of the time, Pallas kernels for 15%

profile of v2, /device:TPU:46, one launch (start us, length us, event | category | flops | bytes accessed | tf_op | source)
XLA Modules:
  0.0 58.6 jit_solution(13430683664253133148)
XLA Ops:
  0.6 0.0 copy-start.3
  0.7 1.9 %shard_map.131.after = bf16[8,80,128]{2,1,0:T(8,128)(2,1)} custom-call(s32[64,512]{1,0:T(8,128)} %bitcast.21, f32[8,64,512]{2,1,0:T(8,128)} %bitcast.11), custom_call_target="tpu_custom_call" | custom-call | tf_op jit(solution)/shard_map/pallas_call | solution.py:413
  2.6 0.0 copy-start.5
  2.6 10.5 %all-to-all-start = ((bf16[8,80,128]{2,1,0:T(8,128)(2,1)}), bf16[8,80,128]{2,1,0:T(8,128)(2,1)S(1)}, u32[]{:S(2)}, u32[]{:S(2)}) async-start(bf16[8,80,128]{2,1,0:T(8,128)(2,1)} %shard_map.131.after), calls=%async_computation | async-start | bytes 327680 | tf_op jit(solution)/shard_map/all_to_all | solution.py:420
  13.1 0.6 copy-done.9
  13.7 0.0 copy-done.10
  13.7 0.0 copy-done.11
  13.7 0.9 %copy-done.6 = bf16[256,256]{1,0:T(8,128)(2,1)S(1)} copy-done((bf16[256,256]{1,0:T(8,128)(2,1)S(1)}, bf16[256,256]{1,0:T(8,128)(2,1)}, u32[]{:S(2)}) %copy-start.6) | copy-done | bytes 131096
  14.6 0.9 %copy-done.7 = bf16[256,256]{1,0:T(8,128)(2,1)S(1)} copy-done((bf16[256,256]{1,0:T(8,128)(2,1)S(1)}, bf16[256,256]{1,0:T(8,128)(2,1)}, u32[]{:S(2)}) %copy-start.7) | copy-done | bytes 131096
  15.5 2.1 %shard_map.132 = (bf16[512,128]{1,0:T(8,128)(2,1)S(1)}, bf16[256,128]{1,0:T(8,128)(2,1)S(1)}, bf16[256,128]{1,0:T(8,128)(2,1)S(1)}, bf16[256,128]{1,0:T(8,128)(2...) custom-call(bf16[8,80,128]{2,1,0:T(8,128)(2,1)S(1)} %copy-done.1, ...), custom_call_target="tpu_custom_call" | custom-call | flops 400000000 | bytes 2000000 | tf_op jit(solution)/shard_map/pallas_call | solution.py:421
  17.6 5.2 %all-to-all-done.got_ref = bf16[8,80,128]{2,1,0:T(8,128)(2,1)S(1)} async-done(((bf16[8,80,128]{2,1,0:T(8,128)(2,1)}), bf16[8,80,128]{2,1,0:T(8,128)(2,1)S(1)}, u32[]{:S(2)}, u32[]{:S(2)}) %all-to-all-start) | async-done | bytes 163872 | tf_op jit(solution)/shard_map/all_to_all | solution.py:420
  22.8 1.3 %shard_map.133 = (bf16[128,1536]{1,0:T(8,128)(2,1)S(1)}, bf16[48,512]{1,0:T(8,128)(2,1)S(1)}, bf16[48,512]{1,0:T(8,128)(2,1)S(1)}, f32[8,8,256]{2,1,0:T(8,128)S(1)}) custom-call(f32[16,256]{1,0:T(8,128)S(1)} %get-tuple-element.26.w_ref, bf16[8,80,128]{2,1,0:T(8,128)(2,1)S(1)} %all-to-all-done.got_ref, bf16[12,64,128]{2,1,0:T(8,128)(2,1)S(1)} %bitcast.16, ...), custom_call_target="tpu_custom_call" | custom-call | tf_op jit(solution)/shard_map/pallas_call | solution.py:435
  24.1 3.2 %collective-permute-start = (bf16[48,512]{1,0:T(8,128)(2,1)S(1)}, bf16[48,512]{1,0:T(8,128)(2,1)S(1)}, u32[]{:S(2)}, u32[]{:S(2)}) collective-permute-start(bf16[48,512]{1,0:T(8,128)(2,1)S(1)} %get-tuple-element.38), channel_id=1, source_target_pairs={{0,1},{1,2},{2,3},{3,4},{4,5},{5,6},{6,7},{7,0},{8,9},{9,10},{10,1... | collective-permute-start | bytes 147464 | tf_op jit(solution)/shard_map/ppermute | solution.py:444
  27.3 2.7 %collective-permute-start.1 = (bf16[48,512]{1,0:T(8,128)(2,1)S(1)}, bf16[48,512]{1,0:T(8,128)(2,1)S(1)}, u32[]{:S(2)}, u32[]{:S(2)}) collective-permute-start(bf16[48,512]{1,0:T(8,128)(2,1)S(1)} %get-tuple-element.39), channel_id=1, source_target_pairs={{0,7},{1,0},{2,1},{3,2},{4,3},{5,4},{6,5},{7,6},{8,15},{9,8},{10,9... | collective-permute-start | bytes 147464 | tf_op jit(solution)/shard_map/ppermute | solution.py:443
  30.0 2.3 %shard_map.134.img_ref = f32[512,256]{1,0:T(8,128)S(1)} custom-call(f32[16,256]{1,0:T(8,128)S(1)} %get-tuple-element.26.w_ref, bf16[128,1536]{1,0:T(8,128)(2,1)S(1)} %get-tuple-element.35.big_ref, bf16[512,128]{1,0:T(8,128)(2,1)S(1)} %get-tuple-element.27.rows_ref, bf16[128,512]{1,0:T(8,128)(2,1)S(1)} %get-tuple-element.36.cols_ref), custom_call_target="tpu_custom_call" | custom-call | flops 2400000000 | bytes 2000000 | tf_op jit(solution)/shard_map/pallas_call | solution.py:445
  32.3 3.1 %collective-permute-done.1.from_right = bf16[48,512]{1,0:T(8,128)(2,1)S(1)} collective-permute-done((bf16[48,512]{1,0:T(8,128)(2,1)S(1)}, bf16[48,512]{1,0:T(8,128)(2,1)S(1)}, u32[]{:S(2)}, u32[]{:S(2)}) %collective-permute-start.1) | collective-permute-done | bytes 49184 | tf_op jit(solution)/shard_map/ppermute | solution.py:443
  35.4 0.1 shard_map.135
  35.5 13.7 %all_to_all.10.got_ref = bf16[8,80,256]{2,1,0:T(8,128)(2,1)S(1)} all-to-all(bf16[8,80,256]{2,1,0:T(8,128)(2,1)S(1)} %shard_map.135), channel_id=1, replica_groups=mesh['depth'=8,'tx'=8,'ty'=8] {'depth'}, dimensions={0} | all-to-all | bytes 655360 | tf_op jit(solution)/shard_map/all_to_all | solution.py:451
  49.2 0.1 shard_map.136
  49.4 0.4 shard_map.137
  49.8 1.9 %collective-permute-start.2 = (bf16[32,640]{1,0:T(8,128)(2,1)S(1)}, bf16[32,640]{1,0:T(8,128)(2,1)S(1)}, u32[]{:S(2)}, u32[]{:S(2)}) collective-permute-start(bf16[32,640]{1,0:T(8,128)(2,1)S(1)} %get-tuple-element.42), channel_id=1, source_target_pairs={{0,8},{8,16},{16,24},{24,32},{32,40},{40,48},{48,56},{56,0},{448,5... | collective-permute-start | bytes 122888 | tf_op jit(solution)/shard_map/ppermute | solution.py:472
  51.7 4.4 %shard_map.138 = (f32[8,64,512]{2,1,0:T(8,128)}, f32[8,64,512]{2,1,0:T(8,128)}, f32[2,8,8,512]{3,2,1,0:T(8,128)S(1)}) custom-call(bf16[8,80,256]{2,1,0:T(8,128)(2,1)S(1)} %all_to_all.10.got_ref, bf16[512,512]{1,0:T(8,128)(2,1)S(1)} %copy-done.2, f32[8,64,512]{2,1,0:T(8,128)S(1)} %bitcast.15, ...), custom_call_target="tpu_custom_call", output_to_operand_aliasing={{0}: (5, {}), {1}: (6, {})} | custom-call | flops 3000000000 | bytes 4000000 | tf_op jit(solution)/shard_map/pallas_call | solution.py:458
  56.2 1.1 %collective-permute-done.2.m_ref = bf16[32,640]{1,0:T(8,128)(2,1)S(1)} collective-permute-done((bf16[32,640]{1,0:T(8,128)(2,1)S(1)}, bf16[32,640]{1,0:T(8,128)(2,1)S(1)}, u32[]{:S(2)}, u32[]{:S(2)}) %collective-permute-start.2) | collective-permute-done | bytes 40992 | tf_op jit(solution)/shard_map/ppermute | solution.py:472
  57.2 1.1 %shard_map.139 = (f32[8,64,512]{2,1,0:T(8,128)}, f32[8,64,512]{2,1,0:T(8,128)}) custom-call(f32[2,8,8,640]{3,2,1,0:T(8,128)S(1)} %get-tuple-element.41.tile_ref, bf16[32,640]{1,0:T(8,128)(2,1)S(1)} %collective-permute-done.2.m_ref, f32[2,8,8,512]{3,2,1,0:T(8,128)S(1)} %get-tuple-element.45.rim_even, ...), custom_call_target="tpu_custom_call", output_to_operand_aliasing={{0}: (4, {}), {1}: (5, {})} | custom-call | tf_op jit(solution)/shard_map/pallas_call | solution.py:475
  (18 shorter events, 0.0 us)
Async XLA Ops:
  0.6 12.4 %copy-start = (f32[8,1,64,512]{3,2,1,0:T(8,128)S(1)}, f32[8,1,64,512]{3,2,1,0:T(8,128)}, u32[]{:S(2)}) copy-start(f32[8,1,64,512]{3,2,1,0:T(8,128)} %param.17) | copy-start | bytes 3145732
  0.6 12.4 %copy-start.3 = (bf16[512,256]{1,0:T(8,128)(2,1)S(1)}, bf16[512,256]{1,0:T(8,128)(2,1)}, u32[]{:S(2)}) copy-start(bf16[512,256]{1,0:T(8,128)(2,1)} %constant.12.clone.cs_in) | copy-start | bytes 786436
  2.6 10.5 %copy-start.1 = (bf16[8,80,128]{2,1,0:T(8,128)(2,1)S(1)}, bf16[8,80,128]{2,1,0:T(8,128)(2,1)}, u32[]{:S(2)}) copy-start(bf16[8,80,128]{2,1,0:T(8,128)(2,1)} %shard_map.131.after) | copy-start | bytes 491524
  2.6 10.5 %copy-start.5 = (bf16[256,256]{1,0:T(8,128)(2,1)S(1)}, bf16[256,256]{1,0:T(8,128)(2,1)}, u32[]{:S(2)}) copy-start(bf16[256,256]{1,0:T(8,128)(2,1)} %constant.15.clone.even_in) | copy-start | bytes 393220
  2.6 10.5 %copy-start.8 = (bf16[16,256]{1,0:T(8,128)(2,1)S(1)}, bf16[16,256]{1,0:T(8,128)(2,1)}, u32[]{:S(2)}) copy-start(bf16[16,256]{1,0:T(8,128)(2,1)} %constant.16.clone.edge_in) | copy-start | bytes 24580
  2.6 20.2 %all-to-all-start = ((bf16[8,80,128]{2,1,0:T(8,128)(2,1)}), bf16[8,80,128]{2,1,0:T(8,128)(2,1)S(1)}, u32[]{:S(2)}, u32[]{:S(2)}) async-start(bf16[8,80,128]{2,1,0:T(8,128)(2,1)} %shard_map.131.after), calls=%async_computation | async-start | bytes 327680 | tf_op jit(solution)/shard_map/all_to_all | solution.py:420
  13.0 0.7 %copy-start.9 = (s32[64]{0:T(128)S(1)}, s32[64]{0:T(128)}, u32[]{:S(2)}) copy-start(s32[64]{0:T(128)} %param.15) | copy-start | bytes 772
  13.1 0.7 %copy-start.10 = (s32[64]{0:T(128)S(1)}, s32[64]{0:T(128)}, u32[]{:S(2)}) copy-start(s32[64]{0:T(128)} %param.16) | copy-start | bytes 772
  13.1 0.7 %copy-start.11 = (f32[12]{0:T(128)S(1)}, f32[12]{0:T(128)}, u32[]{:S(2)}) copy-start(f32[12]{0:T(128)} %w_in.1) | copy-start | bytes 148
  13.7 0.9 %copy-start.6 = (bf16[256,256]{1,0:T(8,128)(2,1)S(1)}, bf16[256,256]{1,0:T(8,128)(2,1)}, u32[]{:S(2)}) copy-start(bf16[256,256]{1,0:T(8,128)(2,1)} %constant.14.clone.lo_in) | copy-start | bytes 393220
  14.6 0.9 %copy-start.7 = (bf16[256,256]{1,0:T(8,128)(2,1)S(1)}, bf16[256,256]{1,0:T(8,128)(2,1)}, u32[]{:S(2)}) copy-start(bf16[256,256]{1,0:T(8,128)(2,1)} %constant.13.clone.hi_in) | copy-start | bytes 393220
  15.5 7.3 %copy-start.4 = (bf16[1,12,64,128]{3,2,1,0:T(8,128)(2,1)S(1)}, bf16[1,12,64,128]{3,2,1,0:T(8,128)(2,1)}, u32[]{:S(2)}) copy-start(bf16[1,12,64,128]{3,2,1,0:T(8,128)(2,1)} %param.13) | copy-start | bytes 589828
  24.1 8.2 %collective-permute-start = (bf16[48,512]{1,0:T(8,128)(2,1)S(1)}, bf16[48,512]{1,0:T(8,128)(2,1)S(1)}, u32[]{:S(2)}, u32[]{:S(2)}) collective-permute-start(bf16[48,512]{1,0:T(8,128)(2,1)S(1)} %get-tuple-element.38), channel_id=1, source_target_pairs={{0,1},{1,2},{2,3},{3,4},{4,5},{5,6},{6,7},{7,0},{8,9},{9,10},{10,1... | collective-permute-start | bytes 147464 | tf_op jit(solution)/shard_map/ppermute | solution.py:444
  27.3 8.1 %collective-permute-start.1 = (bf16[48,512]{1,0:T(8,128)(2,1)S(1)}, bf16[48,512]{1,0:T(8,128)(2,1)S(1)}, u32[]{:S(2)}, u32[]{:S(2)}) collective-permute-start(bf16[48,512]{1,0:T(8,128)(2,1)S(1)} %get-tuple-element.39), channel_id=1, source_target_pairs={{0,7},{1,0},{2,1},{3,2},{4,3},{5,4},{6,5},{7,6},{8,15},{9,8},{10,9... | collective-permute-start | bytes 147464 | tf_op jit(solution)/shard_map/ppermute | solution.py:443
  35.5 13.7 %copy-start.2 = (bf16[512,512]{1,0:T(8,128)(2,1)S(1)}, bf16[512,512]{1,0:T(8,128)(2,1)}, u32[]{:S(2)}) copy-start(bf16[512,512]{1,0:T(8,128)(2,1)} %constant.17.clone.spread_ref) | copy-start | bytes 1572868
  49.8 7.4 %collective-permute-start.2 = (bf16[32,640]{1,0:T(8,128)(2,1)S(1)}, bf16[32,640]{1,0:T(8,128)(2,1)S(1)}, u32[]{:S(2)}, u32[]{:S(2)}) collective-permute-start(bf16[32,640]{1,0:T(8,128)(2,1)S(1)} %get-tuple-element.42), channel_id=1, source_target_pairs={{0,8},{8,16},{16,24},{24,32},{32,40},{40,48},{48,56},{56,0},{448,5... | collective-permute-start | bytes 122888 | tf_op jit(solution)/shard_map/ppermute | solution.py:472

commit v3 on v2

--- a/solution.py
+++ b/solution.py
@@ -126,8 +126,8 @@
     pick_x = picker(bx)
     pick_y = picker(by)
     rows_ref[...] = dot(cs[...], pick_x).astype(BF)
-    xhi_ref[...] = dot(hi_tab[...], pick_x).astype(BF)
-    xlo_ref[...] = dot(lo_tab[...], pick_x).astype(BF)
+    xhi_ref[...] = dot(hi_tab[...], pick_x).T.astype(BF)
+    xlo_ref[...] = dot(lo_tab[...], pick_x).T.astype(BF)
     yhi_ref[...] = dot(hi_tab[...], pick_y).astype(BF)
     ylo_ref[...] = dot(lo_tab[...], pick_y).astype(BF)
     table = dot_tn(pick_y, even[...])
@@ -161,7 +161,7 @@
     summed = dot(coarse, yhi_ref[...]) + dot(coarse, ylo_ref[...])
     hi = summed.astype(BF)
     lo = (summed - hi.astype(F32)).astype(BF)
-    u = (dot_tn(xhi_ref[...], hi) + dot_tn(xhi_ref[...], lo) + dot_tn(xlo_ref[...], hi)) * (1.0 / (TILE * TILE))
+    u = (dot(xhi_ref[...], hi) + dot(xhi_ref[...], lo) + dot(xlo_ref[...], hi)) * (1.0 / (TILE * TILE))
     v = u[:BAND] + sign * pltpu.roll(u[BAND:], BAND, 1)
     v_swap = pltpu.roll(v, BAND, 1)
     coef_a = jnp.where(lane < BAND, v, v_swap)
@@ -181,25 +181,26 @@
     bright = total + pltpu.roll(total, 4, 0)
     place = iota((16, TILE), 0)
     eight = jnp.concatenate([bright, bright], 0)
-    left_ref[0:16, :] = jnp.where(place < 2, eight, 0.0).astype(BF)
-    right_ref[0:16, :] = jnp.where(place < 2, pltpu.roll(eight, 14, 0), 0.0).astype(BF)
-    for ref, cols in ((left_ref, qleft_ref), (right_ref, qright_ref)):
-        ref[16:32, 0:128] = cols[...].astype(BF)
-        ref[16:32, 128:TILE] = jnp.zeros((16, TILE - 128), BF)
+    left_ref[:, 0:TILE] = jnp.where(place < 2, eight, 0.0).astype(BF)
+    right_ref[:, 0:TILE] = jnp.where(place < 2, pltpu.roll(eight, 14, 0), 0.0).astype(BF)
     beyond = (iota((16, 128), 0) & 3) < 2
     heard = [got_ref[p, 64:80, :].astype(F32) for p in range(8)]
-    for p in range(0, 8, 2):
-        pair = [jnp.where(beyond, heard[(d + 1) % 8], heard[(d + 7) % 8]) for d in (p, p + 1)]
-        for d, ring in zip((p, p + 1), pair):
-            ring_ref[d, :, 0:128] = ring[0:8]
-            ring_ref[d, :, 128:256] = ring[8:16]
-        left_ref[32:48, 64 * p : 64 * p + 128] = jnp.concatenate([pair[0][0:8], pair[1][0:8]], 0).astype(BF)
-        right_ref[32:48, 64 * p : 64 * p + 128] = jnp.concatenate([pair[0][8:16], pair[1][8:16]], 0).astype(BF)
+    rings = [jnp.where(beyond, heard[(p + 1) % 8], heard[(p + 7) % 8]) for p in range(8)]
+    for p in range(8):
+        ring_ref[p, :, 0:128] = rings[p][0:8]
+        ring_ref[p, :, 128:HALF] = rings[p][8:16]
+    row, col = iota((16, 128), 0), iota((16, 128), 1)
+    for j, (ref, cols) in enumerate(((left_ref, qleft_ref), (right_ref, qright_ref))):
+        pick = ((col == row + 126 * j) & (row < 2)).astype(BF)
+        ends = dot_nt(pick, jnp.concatenate([ring[8 * j : 8 * j + 8] for ring in rings], 0).astype(BF))
+        both = jnp.concatenate([ends, ends], 1)
+        both = both if j == 0 else pltpu.roll(both, 124, 1)
+        ref[:, TILE:WIDE] = jnp.where(col < STRIP, cols[...], both).astype(BF)
 
 
 def image_kernel(w_ref, big_ref, rows_ref, cols_ref, img_ref):
     count = big_ref.shape[1] // 128
-    chunk = 128
+    chunk = 256
     cols = cols_ref[...]
     for part in range(TILE // chunk):
         half = dot(rows_ref[part * chunk : (part + 1) * chunk, :], big_ref[...]).astype(BF)
@@ -211,10 +212,10 @@
 
 
 def pack_kernel(img_ref, ring_ref, from_left, from_right, out_ref, scr_ref):
-    place = iota((8, TILE), 0)
-    both = jnp.where(place < 2, from_left[0:16, :].astype(F32)[0:8], pltpu.roll(from_right[0:16, :].astype(F32)[0:8], 2, 0))
-    far = from_left[32:48, :].astype(F32)
-    near = from_right[32:48, :].astype(F32)
+    place = iota((8, WIDE), 0)
+    far, near = from_left[...].astype(F32)[0:8], from_right[...].astype(F32)[0:8]
+    both = jnp.where(place < 2, far, pltpu.roll(near, 2, 0))
+    ends, both = both[:, TILE:WIDE], both[:, 0:TILE]
     lane = iota((8, 128), 1)
     for p in range(8):
         base = p * STRIP
@@ -227,9 +228,9 @@
         second = pltpu.roll(both, (TILE - base + CYC) % TILE, 1)[:, 0:128]
         side = jnp.where(lane < 66, first, jnp.where(lane < CYC, second, 0.0))
         scr_ref[2:6, 0:128] = side[0:4]
-        spot, cols = 8 * (p & 1), slice(128 * (p >> 1), 128 * (p >> 1) + 128)
-        corner = jnp.where(lane < STRIP, near[spot : spot + 8, cols], pltpu.roll(far[spot : spot + 8, cols], 4, 0))
-        scr_ref[2:6, 128:HALF] = corner[0:4]
+        first = pltpu.roll(ends, (128 - 8 * p) % 128, 1)
+        second = pltpu.roll(ends, (132 - 8 * p) % 128, 1)
+        scr_ref[2:6, 128:HALF] = jnp.where(lane < 66, first, second)[0:4]
         scr_ref[8:16, :] = ring_ref[p]
         out_ref[p, STRIP:80, :] = scr_ref[...].astype(BF)
 
@@ -243,7 +244,7 @@
 
 
 def quen_side(from_left, from_right):
-    both = [from_left[16:32, 0:128].astype(F32), from_right[16:32, 0:128].astype(F32), jnp.zeros((96, 128), F32)]
+    both = [from_left[:, TILE:WIDE].astype(F32), from_right[:, TILE:WIDE].astype(F32), jnp.zeros((96, 128), F32)]
     return jnp.concatenate(both, 0).T
 
 
@@ -252,41 +253,33 @@
     return jnp.where(behind, pltpu.roll(side, (126 - 2 * z) % 128, 1), pltpu.roll(side, (112 - 2 * z) % 128, 1))
 
 
+def quen_corner(got_ref):
+    return got_ref[:, 64:80, 128:HALF].astype(F32).reshape(16 * PLANES, 128).T[STRIP:CYC]
+
+
 def exposed(intensity):
     return 1.0 - jnp.exp(-DILL_RATE * intensity)
 
 
-def edge_kernel(after, got_ref, spread_ref, quen_in, from_left, from_right, tile_ref, m_ref, near, far, scr, sem):
-    copies = fetch(sem, (quen_in.at[:, pl.ds(0, 8), :], near), (quen_in.at[:, pl.ds(STRIP - 8, 8), :], far))
+def edge_kernel(after, got_ref, spread_ref, m_ref, scr):
     last = lax.axis_index("depth") == 7
-    start = pl.multiple_of(jnp.where(last, STRIP - 16, 0), 16)
-    coarse = [got_ref[z, pl.ds(start, 16), :] for z in range(PLANES)] + [got_ref[z, 64:80, :] for z in range(PLANES)]
-    coarse = jnp.concatenate(coarse, 0)
+    coarse = got_ref[:, 64:80, :].reshape(16 * PLANES, HALF)
     fine = exposed(dot(jnp.concatenate([coarse, coarse], 1), spread_ref[...]))
-    side = acid_side(got_ref)
-    side = exposed(jnp.concatenate([jnp.where(last, side[STRIP - 8 : STRIP], side[0:8]), side[STRIP:CYC]], 0))
-    side_q = quen_side(from_left, from_right)
-    side_q = jnp.where(last, side_q[STRIP - 8 : STRIP], side_q[0:8])
+    side = exposed(acid_side(got_ref)[STRIP:CYC])
+    corner = quen_corner(got_ref)
     for z in range(PLANES):
+        back = fine[16 * z : 16 * z + 8]
         outer = acid_cols(side, z)
-        mine = fine[16 * z : 16 * (z + 1)]
-        tile_ref[0, z, :, 0:TILE] = jnp.where(last, mine[8:16], mine[0:8])
-        tile_ref[0, z, :, TILE:WIDE] = outer[0:8]
-        tile_ref[1, z, :, TILE:WIDE] = quen_cols(side_q, z)
         ring = got_ref[z, 64:80, :].astype(F32)
-        back = fine[128 + 16 * z : 136 + 16 * z]
+        end = acid_cols(corner, z)
         place = slice(2 * z, 2 * z + 2)
         scr[place, 0:TILE] = jnp.where(last, back[0:2], back[6:8])
-        scr[place, TILE:WIDE] = jnp.where(last, outer[8:10], outer[14:16])
+        scr[place, TILE:WIDE] = jnp.where(last, outer[0:2], outer[6:8])
         place = slice(16 + 2 * z, 18 + 2 * z)
         scr[place, 0:HALF] = jnp.where(last, ring[8:10], ring[10:12])
         scr[place, HALF:TILE] = jnp.where(last, ring[12:14], ring[14:16])
-        scr[place, TILE:WIDE] = jnp.where(last, ring[2:4, 128:HALF], ring[4:6, 128:HALF])
+        scr[place, TILE:WIDE] = jnp.where(last, end[0:2], end[6:8])
     m_ref[...] = scr[...].astype(BF)
-    for copy in copies:
-        copy.wait()
-    for z in range(PLANES):
-        tile_ref[1, z, :, 0:TILE] = jnp.where(last, far[z], near[z])
 
 
 def moved(src_a, src_q, z, t, cols):
@@ -312,12 +305,13 @@
 def bake_kernel(
     turn, got_ref, spread_ref, quen_ref, from_left, from_right, *refs,
 ):
-    a_out, q_out, rim_ref, a_ref, q_ref, a_mid, q_mid, a_end, q_end, sem = refs[-10:]
+    a_out, q_out, rim_ref, tile_ref, a_ref, q_ref, a_mid, q_mid, a_end, q_end, sem = refs[-11:]
 
     @pl.when((lax.axis_index("tx") & 1) == turn)
     def _():
         side = exposed(acid_side(got_ref)[0:CYC])
         side_q = quen_side(from_left, from_right)[0:STRIP]
+        corner = quen_corner(got_ref)
         coarse = got_ref[...].reshape(PLANES * 80, HALF)
         fine = dot(jnp.concatenate([coarse, coarse], 1), spread_ref[...])
         for z in range(PLANES):
@@ -326,11 +320,11 @@
             q_ref[z, 0:STRIP, 0:TILE] = quen_ref[z]
             q_ref[z, 0:STRIP, TILE:WIDE] = quen_cols(side_q, z)
             ring = got_ref[z, STRIP:80, :].astype(F32)
-            q_ref[z, STRIP:CYC, :] = jnp.zeros((8, WIDE), F32)
+            q_ref[z, STRIP:CYC, 0:TILE] = jnp.zeros((8, TILE), F32)
+            q_ref[z, STRIP:CYC, TILE:WIDE] = acid_cols(corner, z)
             for i, row in ((0, STRIP), (2, 70)):
                 q_ref[z, row : row + 2, 0:HALF] = ring[8 + i : 10 + i]
                 q_ref[z, row : row + 2, HALF:TILE] = ring[12 + i : 14 + i]
-                q_ref[z, row : row + 2, TILE:WIDE] = ring[2 + i : 4 + i, 128:HALF]
         for z in range(PLANES):
             for t in range(CYC // 8):
                 spot = pl.ds(8 * t, 8)
@@ -350,12 +344,14 @@
             def _():
                 rim_ref[0] = a_end[:, start : start + 8, :]
                 rim_ref[1] = q_end[:, start : start + 8, :]
+                tile_ref[0] = a_ref[:, start : start + 8, :]
+                tile_ref[1] = q_ref[:, start : start + 8, :]
 
         for copy in copies:
             copy.wait()
 
 
-def patch_kernel(tile_ref, m_ref, rim_even, rim_odd, a_in, q_in, a_out, q_out, a_ref, q_ref, a_mid, q_mid, a_end, q_end, sem):
+def patch_kernel(m_ref, rim_even, tile_even, rim_odd, tile_odd, a_in, q_in, a_out, q_out, a_ref, q_ref, a_mid, q_mid, a_end, q_end, sem):
     level = lax.axis_index("depth")
     last = level == 7
 
@@ -366,13 +362,13 @@
         heard = jnp.where(last, row - 2, 5 - row) < 0
         mine = jnp.where(last, row - 6, 1 - row) >= 0
         m = m_ref[...].astype(F32)
+        odd = (lax.axis_index("tx") & 1) == 1
         for z in range(PLANES):
             for f, ref in ((0, a_ref), (1, q_ref)):
                 pair = m[16 * f + 2 * z : 16 * f + 2 * z + 2]
-                ref[z] = jnp.where(heard, jnp.concatenate([pair] * 4, 0), tile_ref[f, z])
+                ref[z] = jnp.where(heard, jnp.concatenate([pair] * 4, 0), jnp.where(odd, tile_odd[f, z], tile_even[f, z]))
         for z in range(PLANES):
             a_mid[z], q_mid[z] = moved(a_ref, q_ref, z, 0, WIDE)
-        odd = (lax.axis_index("tx") & 1) == 1
         for z in range(PLANES):
             a, q = moved(a_mid, q_mid, z, 0, TILE)
             a_end[z] = jnp.where(mine, a, jnp.where(odd, rim_odd[0, z], rim_even[0, z]))
@@ -421,7 +417,7 @@
     *tables, cols, placed, qleft, qright, weight = call(
         table_kernel,
         (
-            shape((TILE, 128), BF), *[shape((256, 128), BF)] * 4, shape((128, TILE), BF),
+            shape((TILE, 128), BF), *[shape((128, 256), BF)] * 2, *[shape((256, 128), BF)] * 2, shape((128, TILE), BF),
             shape((128, 128 * count), BF), shape((16, 128), F32), shape((16, 128), F32), shape((16, HALF), F32),
         ),
         [ANY] + [HBM] * 9,
@@ -435,7 +431,7 @@
     big, left, right, ring = call(
         spectrum_kernel,
         (
-            shape((128, 128 * count), BF), shape((48, TILE), BF), shape((48, TILE), BF),
+            shape((128, 128 * count), BF), shape((16, WIDE), BF), shape((16, WIDE), BF),
             shape((8, 8, HALF), F32),
         ),
         [VMEM] * 11,
@@ -456,26 +452,25 @@
 
     def bake(turn, *before):
         return call(
-            functools.partial(bake_kernel, turn), (out, out, shape((2, PLANES, 8, TILE), F32)),
-            [VMEM] * 5 + [HBM] * len(before), outs=(HBM, HBM, VMEM),
+            functools.partial(bake_kernel, turn), (out, out, shape((2, PLANES, 8, TILE), F32), shape((2, PLANES, 8, WIDE), F32)),
+            [VMEM] * 5 + [HBM] * len(before), outs=(HBM, HBM, VMEM, VMEM),
             scratch=[wide, wide, wide, wide, done, done, dma((2, PLANES))], flops=3_000_000_000, size=4_000_000,
             input_output_aliases={5 + i: i for i in range(len(before))},
         )(planes, con["spread"], quen, from_left, from_right, *before)
 
-    acid, left_over, rim_odd = bake(1)
-    edge, outer = call(
-        edge_kernel, (shape((2, PLANES, 8, WIDE), F32), shape((32, WIDE), BF)), [ANY] + [VMEM] * 2 + [HBM] + [VMEM] * 2,
-        scratch=[tile, tile, pltpu.VMEM((32, WIDE), F32), dma((2,))],
-    )(rim_odd, planes, con["spread"], quen, from_left, from_right)
+    acid, left_over, *odd = bake(1)
+    outer = call(
+        edge_kernel, shape((32, WIDE), BF), [ANY] + [VMEM] * 2, scratch=[pltpu.VMEM((32, WIDE), F32)],
+    )(odd[0], planes, con["spread"])
     end = (n_depth - 1) * n_tx
     pairs = [(t, (t + 1) % n_tx) for t in range(n_tx)] + [(end + t, end + (t - 1) % n_tx) for t in range(n_tx)]
     outer = lax.ppermute(outer, ("depth", "tx"), pairs)
-    acid, left_over, rim_even = bake(0, acid, left_over)
+    acid, left_over, *even = bake(0, acid, left_over)
     low = pltpu.VMEM((PLANES, 8, WIDE), F32)
     acid, left_over = call(
-        patch_kernel, (out, out), [VMEM] * 4 + [HBM] * 2, outs=(HBM, HBM),
-        scratch=[low, low, low, low, tile, tile, dma((2,))], input_output_aliases={4: 0, 5: 1},
-    )(edge, outer, rim_even, rim_odd, acid, left_over)
+        patch_kernel, (out, out), [VMEM] * 5 + [HBM] * 2, outs=(HBM, HBM),
+        scratch=[low, low, low, low, tile, tile, dma((2,))], input_output_aliases={5: 0, 6: 1},
+    )(outer, *even, *odd, acid, left_over)
     return acid[:, None], left_over[:, None]
 
 

time: 58.9 us -> 58.5 us (level)
  no operation moved by 1% of the time
where the time goes in v3:
time: 58.5 us; the launch traced here: 58.1 us
  starting transfers between devices  18.2 us (31%)
  blocking collectives  13.7 us (23%)
  Pallas kernels  13.6 us (23%)
  waiting for transfers between devices  9.33 us (16%)
  local copies, waits for them, and re-layouts  2.46 us (4%)
  between operations  0.81 us (1%)
    all_to_all x1, blocking collectives, on_device(): planes = lax.all_to_all(strips, 'depth', 0, 0, tiled=True)  13.7 us
    all_to_all x1, starting transfers between devices, on_device(): got = lax.all_to_all(packed, 'depth', 0, 0, tiled=True)  10.5 us
    all_to_all x1, waiting for transfers between devices, on_device(): got = lax.all_to_all(packed, 'depth', 0, 0, tiled=True)  5.21 us
    pallas_call x2, Pallas kernels, bake(): call(functools.partial(bake_kernel, turn), (out, out, shape((2, PLANES, 8...  4.4 us
    ppermute x1, starting transfers between devices, on_device(): lax.ppermute(right, 'ty', [(i, (i + 1) % n_ty) for i in range(n_ty)])  3.16 us
    ppermute x1, waiting for transfers between devices, on_device(): lax.ppermute(left, 'ty', [(i, (i - 1) % n_ty) for i in range(n_ty)])  2.88 us
    ppermute x1, starting transfers between devices, on_device(): lax.ppermute(left, 'ty', [(i, (i - 1) % n_ty) for i in range(n_ty)])  2.67 us
    unnamed x24, local copies, waits for them, and re-layouts  2.46 us
  transfers between devices with their start and end apart: 4, of which 3 were waited for; matrix products, arithmetic and copies ran while one was open for 0% of the time, Pallas kernels for 15%

profile of v3, /device:TPU:46, one launch (start us, length us, event | category | flops | bytes accessed | tf_op | source)
XLA Modules:
  0.0 58.1 jit_solution(17595967898895698081)
XLA Ops:
  0.6 0.0 copy-start.3
  0.7 1.9 %shard_map.131.after = bf16[8,80,128]{2,1,0:T(8,128)(2,1)} custom-call(s32[64,512]{1,0:T(8,128)} %bitcast.20, f32[8,64,512]{2,1,0:T(8,128)} %bitcast.11), custom_call_target="tpu_custom_call" | custom-call | tf_op jit(solution)/shard_map/pallas_call | solution.py:409
  2.6 0.0 copy-start.5
  2.6 10.5 %all-to-all-start = ((bf16[8,80,128]{2,1,0:T(8,128)(2,1)}), bf16[8,80,128]{2,1,0:T(8,128)(2,1)S(1)}, u32[]{:S(2)}, u32[]{:S(2)}) async-start(bf16[8,80,128]{2,1,0:T(8,128)(2,1)} %shard_map.131.after), calls=%async_computation | async-start | bytes 327680 | tf_op jit(solution)/shard_map/all_to_all | solution.py:416
  13.1 0.6 copy-done.9
  13.7 0.0 copy-done.10
  13.7 0.0 copy-done.11
  13.7 0.9 %copy-done.6 = bf16[256,256]{1,0:T(8,128)(2,1)S(1)} copy-done((bf16[256,256]{1,0:T(8,128)(2,1)S(1)}, bf16[256,256]{1,0:T(8,128)(2,1)}, u32[]{:S(2)}) %copy-start.6) | copy-done | bytes 131096
  14.6 0.9 %copy-done.7 = bf16[256,256]{1,0:T(8,128)(2,1)S(1)} copy-done((bf16[256,256]{1,0:T(8,128)(2,1)S(1)}, bf16[256,256]{1,0:T(8,128)(2,1)}, u32[]{:S(2)}) %copy-start.7) | copy-done | bytes 131096
  15.5 2.1 %shard_map.132 = (bf16[512,128]{1,0:T(8,128)(2,1)S(1)}, bf16[128,256]{1,0:T(8,128)(2,1)S(1)}, bf16[128,256]{1,0:T(8,128)(2,1)S(1)}, bf16[256,128]{1,0:T(8,128)(2...) custom-call(bf16[8,80,128]{2,1,0:T(8,128)(2,1)S(1)} %copy-done.1, ...), custom_call_target="tpu_custom_call" | custom-call | flops 400000000 | bytes 2000000 | tf_op jit(solution)/shard_map/pallas_call | solution.py:417
  17.6 5.2 %all-to-all-done.got_ref = bf16[8,80,128]{2,1,0:T(8,128)(2,1)S(1)} async-done(((bf16[8,80,128]{2,1,0:T(8,128)(2,1)}), bf16[8,80,128]{2,1,0:T(8,128)(2,1)S(1)}, u32[]{:S(2)}, u32[]{:S(2)}) %all-to-all-start) | async-done | bytes 163872 | tf_op jit(solution)/shard_map/all_to_all | solution.py:416
  22.8 1.5 %shard_map.133 = (bf16[128,1536]{1,0:T(8,128)(2,1)S(1)}, bf16[16,640]{1,0:T(8,128)(2,1)S(1)}, bf16[16,640]{1,0:T(8,128)(2,1)S(1)}, f32[8,8,256]{2,1,0:T(8,128)S(1)}) custom-call(f32[16,256]{1,0:T(8,128)S(1)} %get-tuple-element.26.w_ref, bf16[8,80,128]{2,1,0:T(8,128)(2,1)S(1)} %all-to-all-done.got_ref, bf16[12,64,128]{2,1,0:T(8,128)(2,1)S(1)} %bitcast.15, ...), custom_call_target="tpu_custom_call" | custom-call | tf_op jit(solution)/shard_map/pallas_call | solution.py:431
  24.3 3.2 %collective-permute-start = (bf16[16,640]{1,0:T(8,128)(2,1)S(1)}, bf16[16,640]{1,0:T(8,128)(2,1)S(1)}, u32[]{:S(2)}, u32[]{:S(2)}) collective-permute-start(bf16[16,640]{1,0:T(8,128)(2,1)S(1)} %get-tuple-element.38), channel_id=1, source_target_pairs={{0,1},{1,2},{2,3},{3,4},{4,5},{5,6},{6,7},{7,0},{8,9},{9,10},{10,1... | collective-permute-start | bytes 61448 | tf_op jit(solution)/shard_map/ppermute | solution.py:440
  27.5 2.7 %collective-permute-start.1 = (bf16[16,640]{1,0:T(8,128)(2,1)S(1)}, bf16[16,640]{1,0:T(8,128)(2,1)S(1)}, u32[]{:S(2)}, u32[]{:S(2)}) collective-permute-start(bf16[16,640]{1,0:T(8,128)(2,1)S(1)} %get-tuple-element.39), channel_id=1, source_target_pairs={{0,7},{1,0},{2,1},{3,2},{4,3},{5,4},{6,5},{7,6},{8,15},{9,8},{10,9... | collective-permute-start | bytes 61448 | tf_op jit(solution)/shard_map/ppermute | solution.py:439
  30.1 2.2 %shard_map.134.img_ref = f32[512,256]{1,0:T(8,128)S(1)} custom-call(f32[16,256]{1,0:T(8,128)S(1)} %get-tuple-element.26.w_ref, bf16[128,1536]{1,0:T(8,128)(2,1)S(1)} %get-tuple-element.35.big_ref, bf16[512,128]{1,0:T(8,128)(2,1)S(1)} %get-tuple-element.27.rows_ref, bf16[128,512]{1,0:T(8,128)(2,1)S(1)} %get-tuple-element.36.cols_ref), custom_call_target="tpu_custom_call" | custom-call | flops 2400000000 | bytes 2000000 | tf_op jit(solution)/shard_map/pallas_call | solution.py:441
  32.4 2.9 %collective-permute-done.1.from_right = bf16[16,640]{1,0:T(8,128)(2,1)S(1)} collective-permute-done((bf16[16,640]{1,0:T(8,128)(2,1)S(1)}, bf16[16,640]{1,0:T(8,128)(2,1)S(1)}, u32[]{:S(2)}, u32[]{:S(2)}) %collective-permute-start.1) | collective-permute-done | bytes 20512 | tf_op jit(solution)/shard_map/ppermute | solution.py:439
  35.2 0.1 shard_map.135
  35.4 13.7 %all_to_all.10.got_ref = bf16[8,80,256]{2,1,0:T(8,128)(2,1)S(1)} all-to-all(bf16[8,80,256]{2,1,0:T(8,128)(2,1)S(1)} %shard_map.135), channel_id=1, replica_groups=mesh['depth'=8,'tx'=8,'ty'=8] {'depth'}, dimensions={0} | all-to-all | bytes 655360 | tf_op jit(solution)/shard_map/all_to_all | solution.py:447
  49.1 0.1 shard_map.136
  49.2 0.3 shard_map.137
  49.5 1.9 %collective-permute-start.2 = (bf16[32,640]{1,0:T(8,128)(2,1)S(1)}, bf16[32,640]{1,0:T(8,128)(2,1)S(1)}, u32[]{:S(2)}, u32[]{:S(2)}) collective-permute-start(bf16[32,640]{1,0:T(8,128)(2,1)S(1)} %shard_map.137), channel_id=1, source_target_pairs={{0,8},{8,16},{16,24},{24,32},{32,40},{40,48},{48,56},{56,0},{448,5... | collective-permute-start | bytes 122888 | tf_op jit(solution)/shard_map/ppermute | solution.py:467
  51.4 4.3 %shard_map.138 = (f32[8,64,512]{2,1,0:T(8,128)}, f32[8,64,512]{2,1,0:T(8,128)}, f32[2,8,8,512]{3,2,1,0:T(8,128)S(1)}, f32[2,8,8,640]{3,2,1,0:T(8,128)S(1)}) custom-call(bf16[8,80,256]{2,1,0:T(8,128)(2,1)S(1)} %all_to_all.10.got_ref, bf16[512,512]{1,0:T(8,128)(2,1)S(1)} %copy-done.2, ...), custom_call_target="tpu_custom_call", output_to_operand_aliasing={{0}: (5, {}), {1}: (6, {})} | custom-call | flops 3000000000 | bytes 4000000 | tf_op jit(solution)/shard_map/pallas_call | solution.py:454
  55.7 1.2 %collective-permute-done.2.m_ref = bf16[32,640]{1,0:T(8,128)(2,1)S(1)} collective-permute-done((bf16[32,640]{1,0:T(8,128)(2,1)S(1)}, bf16[32,640]{1,0:T(8,128)(2,1)S(1)}, u32[]{:S(2)}, u32[]{:S(2)}) %collective-permute-start.2) | collective-permute-done | bytes 40992 | tf_op jit(solution)/shard_map/ppermute | solution.py:467
  56.9 1.1 %shard_map.139 = (f32[8,64,512]{2,1,0:T(8,128)}, f32[8,64,512]{2,1,0:T(8,128)}) custom-call(bf16[32,640]{1,0:T(8,128)(2,1)S(1)} %collective-permute-done.2.m_ref, f32[2,8,8,512]{3,2,1,0:T(8,128)S(1)} %get-tuple-element.43.rim_even, f32[2,8,8,640]{3,2,1,0:T(8,128)S(1)} %get-tuple-element.44.tile_even, ...), custom_call_target="tpu_custom_call", output_to_operand_aliasing={{0}: (5, {}), {1}: (6, {})} | custom-call | tf_op jit(solution)/shard_map/pallas_call | solution.py:470
  (18 shorter events, 0.0 us)
Async XLA Ops:
  0.6 12.4 %copy-start = (f32[8,1,64,512]{3,2,1,0:T(8,128)S(1)}, f32[8,1,64,512]{3,2,1,0:T(8,128)}, u32[]{:S(2)}) copy-start(f32[8,1,64,512]{3,2,1,0:T(8,128)} %param.17) | copy-start | bytes 3145732
  0.6 12.4 %copy-start.3 = (bf16[512,256]{1,0:T(8,128)(2,1)S(1)}, bf16[512,256]{1,0:T(8,128)(2,1)}, u32[]{:S(2)}) copy-start(bf16[512,256]{1,0:T(8,128)(2,1)} %constant.12.clone.cs_in) | copy-start | bytes 786436
  2.6 10.5 %copy-start.1 = (bf16[8,80,128]{2,1,0:T(8,128)(2,1)S(1)}, bf16[8,80,128]{2,1,0:T(8,128)(2,1)}, u32[]{:S(2)}) copy-start(bf16[8,80,128]{2,1,0:T(8,128)(2,1)} %shard_map.131.after) | copy-start | bytes 491524
  2.6 10.5 %copy-start.5 = (bf16[256,256]{1,0:T(8,128)(2,1)S(1)}, bf16[256,256]{1,0:T(8,128)(2,1)}, u32[]{:S(2)}) copy-start(bf16[256,256]{1,0:T(8,128)(2,1)} %constant.13.clone.hi_in) | copy-start | bytes 393220
  2.6 10.5 %copy-start.8 = (bf16[16,256]{1,0:T(8,128)(2,1)S(1)}, bf16[16,256]{1,0:T(8,128)(2,1)}, u32[]{:S(2)}) copy-start(bf16[16,256]{1,0:T(8,128)(2,1)} %constant.16.clone.edge_in) | copy-start | bytes 24580
  2.6 20.2 %all-to-all-start = ((bf16[8,80,128]{2,1,0:T(8,128)(2,1)}), bf16[8,80,128]{2,1,0:T(8,128)(2,1)S(1)}, u32[]{:S(2)}, u32[]{:S(2)}) async-start(bf16[8,80,128]{2,1,0:T(8,128)(2,1)} %shard_map.131.after), calls=%async_computation | async-start | bytes 327680 | tf_op jit(solution)/shard_map/all_to_all | solution.py:416
  13.0 0.7 %copy-start.9 = (s32[64]{0:T(128)S(1)}, s32[64]{0:T(128)}, u32[]{:S(2)}) copy-start(s32[64]{0:T(128)} %param.15) | copy-start | bytes 772
  13.1 0.7 %copy-start.10 = (s32[64]{0:T(128)S(1)}, s32[64]{0:T(128)}, u32[]{:S(2)}) copy-start(s32[64]{0:T(128)} %param.16) | copy-start | bytes 772
  13.1 0.7 %copy-start.11 = (f32[12]{0:T(128)S(1)}, f32[12]{0:T(128)}, u32[]{:S(2)}) copy-start(f32[12]{0:T(128)} %w_in.1) | copy-start | bytes 148
  13.7 0.9 %copy-start.6 = (bf16[256,256]{1,0:T(8,128)(2,1)S(1)}, bf16[256,256]{1,0:T(8,128)(2,1)}, u32[]{:S(2)}) copy-start(bf16[256,256]{1,0:T(8,128)(2,1)} %constant.14.clone.lo_in) | copy-start | bytes 393220
  14.6 0.9 %copy-start.7 = (bf16[256,256]{1,0:T(8,128)(2,1)S(1)}, bf16[256,256]{1,0:T(8,128)(2,1)}, u32[]{:S(2)}) copy-start(bf16[256,256]{1,0:T(8,128)(2,1)} %constant.15.clone.even_in) | copy-start | bytes 393220
  15.5 7.3 %copy-start.4 = (bf16[1,12,64,128]{3,2,1,0:T(8,128)(2,1)S(1)}, bf16[1,12,64,128]{3,2,1,0:T(8,128)(2,1)}, u32[]{:S(2)}) copy-start(bf16[1,12,64,128]{3,2,1,0:T(8,128)(2,1)} %param.13) | copy-start | bytes 589828
  24.3 8.1 %collective-permute-start = (bf16[16,640]{1,0:T(8,128)(2,1)S(1)}, bf16[16,640]{1,0:T(8,128)(2,1)S(1)}, u32[]{:S(2)}, u32[]{:S(2)}) collective-permute-start(bf16[16,640]{1,0:T(8,128)(2,1)S(1)} %get-tuple-element.38), channel_id=1, source_target_pairs={{0,1},{1,2},{2,3},{3,4},{4,5},{5,6},{6,7},{7,0},{8,9},{9,10},{10,1... | collective-permute-start | bytes 61448 | tf_op jit(solution)/shard_map/ppermute | solution.py:440
  27.5 7.8 %collective-permute-start.1 = (bf16[16,640]{1,0:T(8,128)(2,1)S(1)}, bf16[16,640]{1,0:T(8,128)(2,1)S(1)}, u32[]{:S(2)}, u32[]{:S(2)}) collective-permute-start(bf16[16,640]{1,0:T(8,128)(2,1)S(1)} %get-tuple-element.39), channel_id=1, source_target_pairs={{0,7},{1,0},{2,1},{3,2},{4,3},{5,4},{6,5},{7,6},{8,15},{9,8},{10,9... | collective-permute-start | bytes 61448 | tf_op jit(solution)/shard_map/ppermute | solution.py:439
  35.4 13.7 %copy-start.2 = (bf16[512,512]{1,0:T(8,128)(2,1)S(1)}, bf16[512,512]{1,0:T(8,128)(2,1)}, u32[]{:S(2)}) copy-start(bf16[512,512]{1,0:T(8,128)(2,1)} %constant.17.clone.spread_ref) | copy-start | bytes 1572868
  49.5 7.4 %collective-permute-start.2 = (bf16[32,640]{1,0:T(8,128)(2,1)S(1)}, bf16[32,640]{1,0:T(8,128)(2,1)S(1)}, u32[]{:S(2)}, u32[]{:S(2)}) collective-permute-start(bf16[32,640]{1,0:T(8,128)(2,1)S(1)} %shard_map.137), channel_id=1, source_target_pairs={{0,8},{8,16},{16,24},{24,32},{32,40},{40,48},{48,56},{56,0},{448,5... | collective-permute-start | bytes 122888 | tf_op jit(solution)/shard_map/ppermute | solution.py:467

commit v4 on v3

--- a/solution.py
+++ b/solution.py
@@ -219,7 +219,7 @@
     lane = iota((8, 128), 1)
     for p in range(8):
         base = p * STRIP
-        out_ref[p, 0:STRIP, :] = img_ref[base : base + STRIP, :].astype(BF)
+        out_ref[7 - p, 0:STRIP, :] = img_ref[base : base + STRIP, :].astype(BF)
         nxt = (base + STRIP) % TILE
         scr_ref[0:2, :] = img_ref[nxt : nxt + 2, :]
         prv = (base - 2) % TILE
@@ -232,7 +232,7 @@
         second = pltpu.roll(ends, (132 - 8 * p) % 128, 1)
         scr_ref[2:6, 128:HALF] = jnp.where(lane < 66, first, second)[0:4]
         scr_ref[8:16, :] = ring_ref[p]
-        out_ref[p, STRIP:80, :] = scr_ref[...].astype(BF)
+        out_ref[7 - p, STRIP:80, :] = scr_ref[...].astype(BF)
 
 
 def acid_side(got_ref):
@@ -240,7 +240,7 @@
 
 
 def acid_cols(side, z):
-    return pltpu.roll(side, (124 - 16 * z) % 128, 1)
+    return pltpu.roll(side, (12 + 16 * z) % 128, 1)
 
 
 def quen_side(from_left, from_right):
@@ -268,9 +268,10 @@
     side = exposed(acid_side(got_ref)[STRIP:CYC])
     corner = quen_corner(got_ref)
     for z in range(PLANES):
-        back = fine[16 * z : 16 * z + 8]
+        seat = 7 - z
+        back = fine[16 * seat : 16 * seat + 8]
         outer = acid_cols(side, z)
-        ring = got_ref[z, 64:80, :].astype(F32)
+        ring = got_ref[seat, 64:80, :].astype(F32)
         end = acid_cols(corner, z)
         place = slice(2 * z, 2 * z + 2)
         scr[place, 0:TILE] = jnp.where(last, back[0:2], back[6:8])
@@ -315,11 +316,12 @@
         coarse = got_ref[...].reshape(PLANES * 80, HALF)
         fine = dot(jnp.concatenate([coarse, coarse], 1), spread_ref[...])
         for z in range(PLANES):
-            a_ref[z, :, 0:TILE] = exposed(fine[80 * z : 80 * z + CYC])
+            seat = 7 - z
+            a_ref[z, :, 0:TILE] = exposed(fine[80 * seat : 80 * seat + CYC])
             a_ref[z, :, TILE:WIDE] = acid_cols(side, z)
             q_ref[z, 0:STRIP, 0:TILE] = quen_ref[z]
             q_ref[z, 0:STRIP, TILE:WIDE] = quen_cols(side_q, z)
-            ring = got_ref[z, STRIP:80, :].astype(F32)
+            ring = got_ref[seat, STRIP:80, :].astype(F32)
             q_ref[z, STRIP:CYC, 0:TILE] = jnp.zeros((8, TILE), F32)
             q_ref[z, STRIP:CYC, TILE:WIDE] = acid_cols(corner, z)
             for i, row in ((0, STRIP), (2, 70)):
@@ -444,7 +446,8 @@
     strips = call(
         pack_kernel, shape((8, 80, HALF), BF), [VMEM] * 4, scratch=[pltpu.VMEM((16, HALF), F32)],
     )(image, ring, from_left, from_right)
-    planes = lax.all_to_all(strips, "depth", 0, 0, tiled=True)
+    seats = list(range(n_depth))[::-1]
+    planes = lax.all_to_all(strips, "depth", 0, 0, tiled=True, axis_index_groups=[seats])
     tile = pltpu.VMEM((PLANES, 8, TILE), F32)
     out = shape((PLANES, STRIP, TILE), F32)
     wide = pltpu.VMEM((PLANES, CYC, WIDE), F32)

time: 58.5 us -> 57.2 us (0.978)
  blocking collectives: 13.7 us -> 12.4 us
    all_to_all x1, blocking collectives: 13.7 us -> 12.4 us  [on_device(): lax.all_to_all(strips, 'depth', 0, 0, tiled=True, axis_index_groups=[seats])]
where the time goes in v4:
time: 57.2 us; the launch traced here: 56.8 us
  starting transfers between devices  18.2 us (32%)
  Pallas kernels  13.6 us (24%)
  blocking collectives  12.4 us (22%)
  waiting for transfers between devices  9.35 us (16%)
  local copies, waits for them, and re-layouts  2.46 us (4%)
  between operations  0.81 us (1%)
    all_to_all x1, blocking collectives, on_device(): lax.all_to_all(strips, 'depth', 0, 0, tiled=True, axis_index_groups=[seats])  12.4 us
    all_to_all x1, starting transfers between devices, on_device(): got = lax.all_to_all(packed, 'depth', 0, 0, tiled=True)  10.5 us
    all_to_all x1, waiting for transfers between devices, on_device(): got = lax.all_to_all(packed, 'depth', 0, 0, tiled=True)  5.21 us
    pallas_call x2, Pallas kernels, bake(): call(functools.partial(bake_kernel, turn), (out, out, shape((2, PLANES, 8...  4.4 us
    ppermute x1, starting transfers between devices, on_device(): lax.ppermute(right, 'ty', [(i, (i + 1) % n_ty) for i in range(n_ty)])  3.16 us
    ppermute x1, waiting for transfers between devices, on_device(): lax.ppermute(left, 'ty', [(i, (i - 1) % n_ty) for i in range(n_ty)])  2.88 us
    ppermute x1, starting transfers between devices, on_device(): lax.ppermute(left, 'ty', [(i, (i - 1) % n_ty) for i in range(n_ty)])  2.67 us
    unnamed x24, local copies, waits for them, and re-layouts  2.46 us
  transfers between devices with their start and end apart: 4, of which 3 were waited for; matrix products, arithmetic and copies ran while one was open for 0% of the time, Pallas kernels for 15%

profile of v4, /device:TPU:46, one launch (start us, length us, event | category | flops | bytes accessed | tf_op | source)
XLA Modules:
  0.0 56.8 jit_solution(12585544305425055829)
XLA Ops:
  0.6 0.0 copy-start.3
  0.7 1.9 %shard_map.131.after = bf16[8,80,128]{2,1,0:T(8,128)(2,1)} custom-call(s32[64,512]{1,0:T(8,128)} %bitcast.20, f32[8,64,512]{2,1,0:T(8,128)} %bitcast.11), custom_call_target="tpu_custom_call" | custom-call | tf_op jit(solution)/shard_map/pallas_call | solution.py:411
  2.6 0.0 copy-start.5
  2.6 10.5 %all-to-all-start = ((bf16[8,80,128]{2,1,0:T(8,128)(2,1)}), bf16[8,80,128]{2,1,0:T(8,128)(2,1)S(1)}, u32[]{:S(2)}, u32[]{:S(2)}) async-start(bf16[8,80,128]{2,1,0:T(8,128)(2,1)} %shard_map.131.after), calls=%async_computation | async-start | bytes 327680 | tf_op jit(solution)/shard_map/all_to_all | solution.py:418
  13.1 0.6 %copy-done.9 = s32[64]{0:T(128)S(1)} copy-done((s32[64]{0:T(128)S(1)}, s32[64]{0:T(128)}, u32[]{:S(2)}) %copy-start.9) | copy-done | bytes 280
  13.7 0.0 copy-done.10
  13.7 0.0 copy-done.11
  13.7 0.9 %copy-done.6 = bf16[256,256]{1,0:T(8,128)(2,1)S(1)} copy-done((bf16[256,256]{1,0:T(8,128)(2,1)S(1)}, bf16[256,256]{1,0:T(8,128)(2,1)}, u32[]{:S(2)}) %copy-start.6) | copy-done | bytes 131096
  14.6 0.9 %copy-done.7 = bf16[256,256]{1,0:T(8,128)(2,1)S(1)} copy-done((bf16[256,256]{1,0:T(8,128)(2,1)S(1)}, bf16[256,256]{1,0:T(8,128)(2,1)}, u32[]{:S(2)}) %copy-start.7) | copy-done | bytes 131096
  15.5 2.1 %shard_map.132 = (bf16[512,128]{1,0:T(8,128)(2,1)S(1)}, bf16[128,256]{1,0:T(8,128)(2,1)S(1)}, bf16[128,256]{1,0:T(8,128)(2,1)S(1)}, bf16[256,128]{1,0:T(8,128)(2...) custom-call(bf16[8,80,128]{2,1,0:T(8,128)(2,1)S(1)} %copy-done.1, ...), custom_call_target="tpu_custom_call" | custom-call | flops 400000000 | bytes 2000000 | tf_op jit(solution)/shard_map/pallas_call | solution.py:419
  17.6 5.2 %all-to-all-done.got_ref = bf16[8,80,128]{2,1,0:T(8,128)(2,1)S(1)} async-done(((bf16[8,80,128]{2,1,0:T(8,128)(2,1)}), bf16[8,80,128]{2,1,0:T(8,128)(2,1)S(1)}, u32[]{:S(2)}, u32[]{:S(2)}) %all-to-all-start) | async-done | bytes 163872 | tf_op jit(solution)/shard_map/all_to_all | solution.py:418
  22.8 1.5 %shard_map.133 = (bf16[128,1536]{1,0:T(8,128)(2,1)S(1)}, bf16[16,640]{1,0:T(8,128)(2,1)S(1)}, bf16[16,640]{1,0:T(8,128)(2,1)S(1)}, f32[8,8,256]{2,1,0:T(8,128)S(1)}) custom-call(f32[16,256]{1,0:T(8,128)S(1)} %get-tuple-element.26.w_ref, bf16[8,80,128]{2,1,0:T(8,128)(2,1)S(1)} %all-to-all-done.got_ref, bf16[12,64,128]{2,1,0:T(8,128)(2,1)S(1)} %bitcast.15, ...), custom_call_target="tpu_custom_call" | custom-call | tf_op jit(solution)/shard_map/pallas_call | solution.py:433
  24.3 3.2 %collective-permute-start = (bf16[16,640]{1,0:T(8,128)(2,1)S(1)}, bf16[16,640]{1,0:T(8,128)(2,1)S(1)}, u32[]{:S(2)}, u32[]{:S(2)}) collective-permute-start(bf16[16,640]{1,0:T(8,128)(2,1)S(1)} %get-tuple-element.38), channel_id=1, source_target_pairs={{0,1},{1,2},{2,3},{3,4},{4,5},{5,6},{6,7},{7,0},{8,9},{9,10},{10,1... | collective-permute-start | bytes 61448 | tf_op jit(solution)/shard_map/ppermute | solution.py:442
  27.5 2.7 %collective-permute-start.1 = (bf16[16,640]{1,0:T(8,128)(2,1)S(1)}, bf16[16,640]{1,0:T(8,128)(2,1)S(1)}, u32[]{:S(2)}, u32[]{:S(2)}) collective-permute-start(bf16[16,640]{1,0:T(8,128)(2,1)S(1)} %get-tuple-element.39), channel_id=1, source_target_pairs={{0,7},{1,0},{2,1},{3,2},{4,3},{5,4},{6,5},{7,6},{8,15},{9,8},{10,9... | collective-permute-start | bytes 61448 | tf_op jit(solution)/shard_map/ppermute | solution.py:441
  30.1 2.2 %shard_map.134.img_ref = f32[512,256]{1,0:T(8,128)S(1)} custom-call(f32[16,256]{1,0:T(8,128)S(1)} %get-tuple-element.26.w_ref, bf16[128,1536]{1,0:T(8,128)(2,1)S(1)} %get-tuple-element.35.big_ref, bf16[512,128]{1,0:T(8,128)(2,1)S(1)} %get-tuple-element.27.rows_ref, bf16[128,512]{1,0:T(8,128)(2,1)S(1)} %get-tuple-element.36.cols_ref), custom_call_target="tpu_custom_call" | custom-call | flops 2400000000 | bytes 2000000 | tf_op jit(solution)/shard_map/pallas_call | solution.py:443
  32.4 2.9 %collective-permute-done.1.from_right = bf16[16,640]{1,0:T(8,128)(2,1)S(1)} collective-permute-done((bf16[16,640]{1,0:T(8,128)(2,1)S(1)}, bf16[16,640]{1,0:T(8,128)(2,1)S(1)}, u32[]{:S(2)}, u32[]{:S(2)}) %collective-permute-start.1) | collective-permute-done | bytes 20512 | tf_op jit(solution)/shard_map/ppermute | solution.py:441
  35.2 0.1 shard_map.135
  35.4 12.4 %all_to_all.10.got_ref = bf16[8,80,256]{2,1,0:T(8,128)(2,1)S(1)} all-to-all(bf16[8,80,256]{2,1,0:T(8,128)(2,1)S(1)} %shard_map.135), channel_id=1, replica_groups={{448,384,320,256,192,128,64,0},{449,385,321,257,193,129,65,1},{450,386,..., dimensions={0} | all-to-all | bytes 655360 | tf_op jit(solution)/shard_map/all_to_all | solution.py:450
  47.8 0.1 shard_map.136
  48.0 0.3 shard_map.137
  48.2 1.9 %collective-permute-start.2 = (bf16[32,640]{1,0:T(8,128)(2,1)S(1)}, bf16[32,640]{1,0:T(8,128)(2,1)S(1)}, u32[]{:S(2)}, u32[]{:S(2)}) collective-permute-start(bf16[32,640]{1,0:T(8,128)(2,1)S(1)} %shard_map.137), channel_id=1, source_target_pairs={{0,8},{8,16},{16,24},{24,32},{32,40},{40,48},{48,56},{56,0},{448,5... | collective-permute-start | bytes 122888 | tf_op jit(solution)/shard_map/ppermute | solution.py:470
  50.2 4.3 %shard_map.138 = (f32[8,64,512]{2,1,0:T(8,128)}, f32[8,64,512]{2,1,0:T(8,128)}, f32[2,8,8,512]{3,2,1,0:T(8,128)S(1)}, f32[2,8,8,640]{3,2,1,0:T(8,128)S(1)}) custom-call(bf16[8,80,256]{2,1,0:T(8,128)(2,1)S(1)} %all_to_all.10.got_ref, bf16[512,512]{1,0:T(8,128)(2,1)S(1)} %copy-done.2, ...), custom_call_target="tpu_custom_call", output_to_operand_aliasing={{0}: (5, {}), {1}: (6, {})} | custom-call | flops 3000000000 | bytes 4000000 | tf_op jit(solution)/shard_map/pallas_call | solution.py:457
  54.4 1.2 %collective-permute-done.2.m_ref = bf16[32,640]{1,0:T(8,128)(2,1)S(1)} collective-permute-done((bf16[32,640]{1,0:T(8,128)(2,1)S(1)}, bf16[32,640]{1,0:T(8,128)(2,1)S(1)}, u32[]{:S(2)}, u32[]{:S(2)}) %collective-permute-start.2) | collective-permute-done | bytes 40992 | tf_op jit(solution)/shard_map/ppermute | solution.py:470
  55.7 1.1 %shard_map.139 = (f32[8,64,512]{2,1,0:T(8,128)}, f32[8,64,512]{2,1,0:T(8,128)}) custom-call(bf16[32,640]{1,0:T(8,128)(2,1)S(1)} %collective-permute-done.2.m_ref, f32[2,8,8,512]{3,2,1,0:T(8,128)S(1)} %get-tuple-element.43.rim_even, f32[2,8,8,640]{3,2,1,0:T(8,128)S(1)} %get-tuple-element.44.tile_even, ...), custom_call_target="tpu_custom_call", output_to_operand_aliasing={{0}: (5, {}), {1}: (6, {})} | custom-call | tf_op jit(solution)/shard_map/pallas_call | solution.py:473
  (18 shorter events, 0.0 us)
Async XLA Ops:
  0.6 12.4 %copy-start = (f32[8,1,64,512]{3,2,1,0:T(8,128)S(1)}, f32[8,1,64,512]{3,2,1,0:T(8,128)}, u32[]{:S(2)}) copy-start(f32[8,1,64,512]{3,2,1,0:T(8,128)} %param.17) | copy-start | bytes 3145732
  0.6 12.4 %copy-start.3 = (bf16[512,256]{1,0:T(8,128)(2,1)S(1)}, bf16[512,256]{1,0:T(8,128)(2,1)}, u32[]{:S(2)}) copy-start(bf16[512,256]{1,0:T(8,128)(2,1)} %constant.12.clone.cs_in) | copy-start | bytes 786436
  2.6 10.5 %copy-start.1 = (bf16[8,80,128]{2,1,0:T(8,128)(2,1)S(1)}, bf16[8,80,128]{2,1,0:T(8,128)(2,1)}, u32[]{:S(2)}) copy-start(bf16[8,80,128]{2,1,0:T(8,128)(2,1)} %shard_map.131.after) | copy-start | bytes 491524
  2.6 10.5 %copy-start.5 = (bf16[256,256]{1,0:T(8,128)(2,1)S(1)}, bf16[256,256]{1,0:T(8,128)(2,1)}, u32[]{:S(2)}) copy-start(bf16[256,256]{1,0:T(8,128)(2,1)} %constant.13.clone.hi_in) | copy-start | bytes 393220
  2.6 10.5 %copy-start.8 = (bf16[16,256]{1,0:T(8,128)(2,1)S(1)}, bf16[16,256]{1,0:T(8,128)(2,1)}, u32[]{:S(2)}) copy-start(bf16[16,256]{1,0:T(8,128)(2,1)} %constant.16.clone.edge_in) | copy-start | bytes 24580
  2.6 20.2 %all-to-all-start = ((bf16[8,80,128]{2,1,0:T(8,128)(2,1)}), bf16[8,80,128]{2,1,0:T(8,128)(2,1)S(1)}, u32[]{:S(2)}, u32[]{:S(2)}) async-start(bf16[8,80,128]{2,1,0:T(8,128)(2,1)} %shard_map.131.after), calls=%async_computation | async-start | bytes 327680 | tf_op jit(solution)/shard_map/all_to_all | solution.py:418
  13.0 0.7 %copy-start.9 = (s32[64]{0:T(128)S(1)}, s32[64]{0:T(128)}, u32[]{:S(2)}) copy-start(s32[64]{0:T(128)} %param.15) | copy-start | bytes 772
  13.1 0.7 %copy-start.10 = (s32[64]{0:T(128)S(1)}, s32[64]{0:T(128)}, u32[]{:S(2)}) copy-start(s32[64]{0:T(128)} %param.16) | copy-start | bytes 772
  13.1 0.7 %copy-start.11 = (f32[12]{0:T(128)S(1)}, f32[12]{0:T(128)}, u32[]{:S(2)}) copy-start(f32[12]{0:T(128)} %w_in.1) | copy-start | bytes 148
  13.7 0.9 %copy-start.6 = (bf16[256,256]{1,0:T(8,128)(2,1)S(1)}, bf16[256,256]{1,0:T(8,128)(2,1)}, u32[]{:S(2)}) copy-start(bf16[256,256]{1,0:T(8,128)(2,1)} %constant.14.clone.lo_in) | copy-start | bytes 393220
  14.6 0.9 %copy-start.7 = (bf16[256,256]{1,0:T(8,128)(2,1)S(1)}, bf16[256,256]{1,0:T(8,128)(2,1)}, u32[]{:S(2)}) copy-start(bf16[256,256]{1,0:T(8,128)(2,1)} %constant.15.clone.even_in) | copy-start | bytes 393220
  15.5 7.3 %copy-start.4 = (bf16[1,12,64,128]{3,2,1,0:T(8,128)(2,1)S(1)}, bf16[1,12,64,128]{3,2,1,0:T(8,128)(2,1)}, u32[]{:S(2)}) copy-start(bf16[1,12,64,128]{3,2,1,0:T(8,128)(2,1)} %param.13) | copy-start | bytes 589828
  24.3 8.1 %collective-permute-start = (bf16[16,640]{1,0:T(8,128)(2,1)S(1)}, bf16[16,640]{1,0:T(8,128)(2,1)S(1)}, u32[]{:S(2)}, u32[]{:S(2)}) collective-permute-start(bf16[16,640]{1,0:T(8,128)(2,1)S(1)} %get-tuple-element.38), channel_id=1, source_target_pairs={{0,1},{1,2},{2,3},{3,4},{4,5},{5,6},{6,7},{7,0},{8,9},{9,10},{10,1... | collective-permute-start | bytes 61448 | tf_op jit(solution)/shard_map/ppermute | solution.py:442
  27.5 7.8 %collective-permute-start.1 = (bf16[16,640]{1,0:T(8,128)(2,1)S(1)}, bf16[16,640]{1,0:T(8,128)(2,1)S(1)}, u32[]{:S(2)}, u32[]{:S(2)}) collective-permute-start(bf16[16,640]{1,0:T(8,128)(2,1)S(1)} %get-tuple-element.39), channel_id=1, source_target_pairs={{0,7},{1,0},{2,1},{3,2},{4,3},{5,4},{6,5},{7,6},{8,15},{9,8},{10,9... | collective-permute-start | bytes 61448 | tf_op jit(solution)/shard_map/ppermute | solution.py:441
  35.4 12.4 %copy-start.2 = (bf16[512,512]{1,0:T(8,128)(2,1)S(1)}, bf16[512,512]{1,0:T(8,128)(2,1)}, u32[]{:S(2)}) copy-start(bf16[512,512]{1,0:T(8,128)(2,1)} %constant.17.clone.spread_ref) | copy-start | bytes 1572868
  48.2 7.4 %collective-permute-start.2 = (bf16[32,640]{1,0:T(8,128)(2,1)S(1)}, bf16[32,640]{1,0:T(8,128)(2,1)S(1)}, u32[]{:S(2)}, u32[]{:S(2)}) collective-permute-start(bf16[32,640]{1,0:T(8,128)(2,1)S(1)} %shard_map.137), channel_id=1, source_target_pairs={{0,8},{8,16},{16,24},{24,32},{32,40},{40,48},{48,56},{56,0},{448,5... | collective-permute-start | bytes 122888 | tf_op jit(solution)/shard_map/ppermute | solution.py:470
